TPU v7x, 32 devices: a whole 2x2x4 slice. The times are simulated.
32 devices in a mesh: cfg: 2 (over y), seq: 16 (over z, x, core).
Axes of the slice: x: 2, y: 2, z: 4, core: 2. Of those that a mesh axis runs over, the one named last changes fastest.
Arguments:
- hidden: bfloat16 [2, 768, 3072], P('cfg', 'seq'), may hold values from -3 to 3
- queries: bfloat16 [2, 768, 2048], P('cfg', 'seq'), may hold values from -5 to 5
- key_proj: bfloat16 [2, 768, 2048], P('cfg', 'seq'), may hold values from -5 to 5
- value_proj: bfloat16 [2, 768, 2048], P('cfg', 'seq'), may hold values from -12 to 12
- norm_gain: float32 [2, 64], replicated, may hold values from 0.1 to 1.9
- norm_bias: float32 [2, 64], replicated, may hold values from -2 to 2
- positions: int32 [3, 768], P(None, 'seq'), may hold values from 0 to 47
- text_len: int32 [2], P('cfg'), may hold values from 1 to 226
- time_embed: bfloat16 [512], replicated, may hold values from -6 to 6
- gate_table: bfloat16 [512, 3072], P(None, 'seq'), may hold values from -0.25 to 0.25
- mod_table: bfloat16 [512, 6144], P(None, 'seq'), may hold values from -0.25 to 0.25
- out_weight: bfloat16 [2048, 3072], P(None, ('cfg', 'seq')), may hold values from -0.125 to 0.125
- proj_weight: bfloat16 [3072, 64], replicated, may hold values from -0.109375 to 0.109375
- proj_bias: float32 [64], replicated, may hold values from -3 to 3
- latent: float32 [768, 64], P('seq'), may hold values from -6 to 6
- solver_coef: float32 [2, 50], replicated, may hold values from 0.3 to 1.2
- step_index: int32 [1], replicated, may hold values from 0 to 49
Outputs:
- latent_next: float32 [768, 64], P('seq', 'cfg')
All inputs are finite; a program needn't handle non-finite values.
Results may differ from a plain program's by a relative error of at most 0.0072.
Values may be sent and summed in bfloat16 or wider, within the bound.
A program may use at most 128 MiB of HBM per device.

v0:
```python
import math

import jax
import jax.numpy as jnp
import numpy as np
from jax import lax
from jax.sharding import PartitionSpec as P

TEXT_SLOTS = 256


GUIDANCE = 6.0


def swapped(value, axis, bit):
    return lax.ppermute(value, axis, [(i, i ^ 1 << bit) for i in range(lax.axis_size(axis))])


def layer_norm(values, epsilon):
    centre = jnp.mean(values, axis=-1, keepdims=True)
    centred = values - centre
    variance = jnp.mean(centred * centred, axis=-1, keepdims=True)
    return centred * lax.rsqrt(variance + epsilon)


def rotary_angles(positions):
    pos_float = positions.astype(jnp.float32)
    time_freq = jnp.asarray(10000.0 ** (-2.0 * np.arange(8) / 16.0), jnp.float32)
    space_freq = jnp.asarray(10000.0 ** (-2.0 * np.arange(12) / 24.0), jnp.float32)
    return jnp.concatenate(
        [
            pos_float[0][:, None] * time_freq[None, :],
            pos_float[1][:, None] * space_freq[None, :],
            pos_float[2][:, None] * space_freq[None, :],
        ],
        axis=1,
    )


def norm_rotate(values, gain_row, offset, angles, is_video):
    row_count = values.shape[0]
    head_count = values.shape[1] // 64
    normed = (
        layer_norm(values.astype(jnp.float32).reshape(row_count, head_count, 64), 1e-06) * gain_row
        + offset
    )
    paired = normed.reshape(row_count, head_count, 32, 2)
    first_half = paired[..., 0]
    second = paired[..., 1]
    cosine = jnp.cos(angles)[:, None, :]
    sine_part = jnp.sin(angles)[:, None, :]
    rotated = jnp.stack(
        [first_half * cosine - second * sine_part, first_half * sine_part + second * cosine],
        axis=-1,
    ).reshape(row_count, head_count, 64)
    return jnp.where(is_video[:, None, None], rotated, normed).astype(jnp.bfloat16)


def on_device(
    hidden,
    queries,
    key_proj,
    value_proj,
    norm_gain,
    norm_bias,
    positions,
    text_len,
    time_embed,
    gate_table,
    mod_table,
    out_weight,
    proj_weight,
    proj_bias,
    latent,
    solver_coef,
    step_index,
):
    seq_count = lax.axis_size("seq")
    seq_place = lax.axis_index("seq")
    local_rows = queries.shape[1]
    head_count = queries.shape[2] // 64
    head_group = max(head_count // seq_count, 1)
    row_split = max(seq_count // head_count, 1)
    part_rows = local_rows // row_split
    head_sets = head_count // head_group
    row_index = seq_place * local_rows + jnp.arange(local_rows)
    is_video = row_index >= TEXT_SLOTS
    angles = rotary_angles(positions)
    rot_query = norm_rotate(queries[0], norm_gain[0], norm_bias[0], angles, is_video)
    rot_key = norm_rotate(key_proj[0], norm_gain[1], norm_bias[1], angles, is_video)
    query_send = rot_query.reshape(row_split, part_rows, head_sets, head_group, 64)
    query_send = query_send.transpose(2, 0, 1, 3, 4).reshape(seq_count, part_rows * head_group * 64)

    def spread(values):
        grouped = values.reshape(local_rows, head_sets, head_group * 64).transpose(1, 0, 2)
        widened = jnp.broadcast_to(
            grouped[:, None], (head_sets, row_split, local_rows, head_group * 64)
        )
        return widened.reshape(seq_count, local_rows * head_group * 64)

    key_send = spread(rot_key)
    value_send = spread(value_proj[0].reshape(local_rows, head_count, 64))
    query_recv, key_recv, value_recv = (
        lax.all_to_all(query_send, "seq", split_axis=0, concat_axis=0, tiled=True),
        lax.all_to_all(key_send, "seq", split_axis=0, concat_axis=0, tiled=True),
        lax.all_to_all(value_send, "seq", split_axis=0, concat_axis=0, tiled=True),
    )
    total_keys = seq_count * local_rows
    query_count = seq_count * part_rows
    query_all = query_recv.reshape(query_count, head_group, 64)
    key_index = jnp.arange(total_keys)
    key_valid = (key_index >= TEXT_SLOTS) | (key_index < text_len[0])
    block_keys = math.gcd(512, total_keys)
    block_count = total_keys // block_keys

    def key_step(state_pair, operands):
        numerator, denominator = state_pair
        key_block, value_block, valid_block = operands
        scores = (
            jnp.einsum("qgd,kgd->gqk", query_all, key_block, preferred_element_type=jnp.float32)
            * 0.125
        )
        weights = jnp.where(valid_block[None, None, :], jnp.exp(scores), 0.0)
        denominator = denominator + jnp.sum(weights, axis=2)
        numerator = numerator + jnp.einsum(
            "gqk,kgd->gqd",
            weights.astype(jnp.bfloat16),
            value_block,
            preferred_element_type=jnp.float32,
        )
        return ((numerator, denominator), None)

    start_state = (
        jnp.zeros((head_group, query_count, 64), jnp.float32),
        jnp.zeros((head_group, query_count), jnp.float32),
    )
    scanned = (
        key_recv.reshape(block_count, block_keys, head_group, 64),
        value_recv.reshape(block_count, block_keys, head_group, 64),
        key_valid.reshape(block_count, block_keys),
    )
    final_state, unused_out = lax.scan(key_step, start_state, scanned)
    attended = (final_state[0] / final_state[1][..., None]).astype(jnp.bfloat16)
    back_send = attended.reshape(head_group, seq_count, part_rows, 64).transpose(1, 2, 0, 3)
    back_send = back_send.reshape(seq_count, part_rows * head_group * 64)
    back_recv = lax.all_to_all(back_send, "seq", split_axis=0, concat_axis=0, tiled=True)
    attended_rows = back_recv.reshape(head_sets, row_split, part_rows, head_group, 64)
    attended_rows = attended_rows.transpose(1, 2, 0, 3, 4).reshape(local_rows, head_count * 64)
    embed_act = jax.nn.silu(time_embed.astype(jnp.float32)).astype(jnp.bfloat16)[None, :]
    gate_full, mod_full = (
        lax.all_gather(gate_table, "seq", axis=1, tiled=True),
        lax.all_gather(mod_table, "seq", axis=1, tiled=True),
    )
    gate_vec = jnp.dot(embed_act, gate_full, preferred_element_type=jnp.float32)[0]
    modulation = jnp.dot(embed_act, mod_full, preferred_element_type=jnp.float32)[0]
    projected = jnp.dot(
        attended_rows,
        lax.all_gather(out_weight, ("cfg", "seq"), axis=1, tiled=True),
        preferred_element_type=jnp.float32,
    )
    model_width = hidden.shape[2]
    residual = hidden[0].astype(jnp.float32) + gate_vec[None, :] * projected
    normed = (
        layer_norm(residual, 1e-05) * (1.0 + modulation[model_width:]) + modulation[:model_width]
    )
    normed = normed.astype(jnp.bfloat16)
    prediction = jnp.dot(normed, proj_weight, preferred_element_type=jnp.float32) + proj_bias
    cfg_place = lax.axis_index("cfg")
    own_width = prediction.shape[1] // 2
    own_pred = lax.dynamic_slice_in_dim(prediction, cfg_place * own_width, own_width, 1)
    sent_pred = lax.dynamic_slice_in_dim(prediction, (1 - cfg_place) * own_width, own_width, 1)
    partner = swapped(sent_pred, "cfg", 0)
    is_cond = cfg_place == 0
    cond_pred = jnp.where(is_cond, own_pred, partner)
    uncond_pred = jnp.where(is_cond, partner, own_pred)
    guided = uncond_pred + GUIDANCE * (cond_pred - uncond_pred)
    own_latent = lax.dynamic_slice_in_dim(latent, cfg_place * own_width, own_width, 1)
    step_coefs = lax.dynamic_index_in_dim(solver_coef, step_index[0], axis=1, keepdims=False)
    updated = step_coefs[0] * own_latent + step_coefs[1] * guided
    return jnp.where(is_video[:, None], updated, 0.0)


def solution(mesh):
    placed = (
        P("cfg", "seq", None),
        P("cfg", "seq", None),
        P("cfg", "seq", None),
        P("cfg", "seq", None),
        P(),
        P(),
        P(None, "seq"),
        P("cfg"),
        P(),
        P(None, "seq"),
        P(None, "seq"),
        P(None, ("cfg", "seq")),
        P(),
        P(),
        P("seq", None),
        P(),
        P(),
    )
    return jax.shard_map(
        on_device, mesh=mesh, in_specs=placed, out_specs=P("seq", "cfg"), check_vma=False
    )
```

profile of v0, /device:TPU:3, one launch (start us, length us, event | category | flops | bytes accessed | tf_op | source)
XLA Modules:
  0.0 246.8 jit_solution(3474995947418459851)
XLA Ops:
  8.8 1.2 copy.35
  12.5 0.8 multiply_add_fusion.1
  13.3 0.8 multiply_add_fusion
  14.2 3.5 %multiply_subtract_fusion = (bf16[48,32,32,1]{0,3,2,1:T(2,128)(2,1)S(1)}, bf16[48,32,32,1]{0,3,2,1:T(2,128)(2,1)S(1)}, bf16[48,32,32,1]{0,3,2,1:T(2,128)(2,1)S(1)}, bf16[48,32,32,1]{0,3,2,1:T(2,128)(2,1)}) fusion(f32[48,32,32,2]{0,3,2,1:T(2,128)S(1)} %multiply_add_fusion, f32[48,32]{0,1:T(8,128)S(1)} %get-tuple-element.112, ...), kind=kLoop, calls=%fused_computation.33 | loop fusion | flops 786432 | bytes 1191936 | tf_op jit(solution)/shard_map/sub | solution.py:53
  17.7 1.4 pad_maximum_fusion.1
  20.6 1.7 reduce.23
  22.3 0.8 reshape.348
  23.1 6.7 %all-to-all-start.1 = ((bf16[16,2,3072]{2,1,0:T(2,128)(2,1)}), bf16[16,2,3072]{2,1,0:T(2,128)(2,1)S(1)}, u32[]{:S(2)}, u32[]{:S(2)}) async-start(bf16[16,2,3072]{2,1,0:T(2,128)(2,1)} %reshape.348), calls=%async_computation.1 | async-start | bytes 393216 | tf_op jit(solution)/shard_map/all_to_all | solution.py:104
  29.8 2.4 pad_maximum_fusion
  33.3 1.7 reduce.22
  35.0 0.8 reshape.346
  35.8 1.1 all-to-all-done.1
  37.0 5.2 %all-to-all-start = ((bf16[16,2,3072]{2,1,0:T(2,128)(2,1)}), bf16[16,2,3072]{2,1,0:T(2,128)(2,1)S(1)}, u32[]{:S(2)}, u32[]{:S(2)}) async-start(bf16[16,2,3072]{2,1,0:T(2,128)(2,1)} %reshape.346), calls=%async_computation | async-start | bytes 393216 | tf_op jit(solution)/shard_map/all_to_all | solution.py:105
  42.4 1.7 reduce.24
  44.9 8.1 %all-to-all-done = bf16[16,2,3072]{2,1,0:T(2,128)(2,1)S(1)} async-done(((bf16[16,2,3072]{2,1,0:T(2,128)(2,1)}), bf16[16,2,3072]{2,1,0:T(2,128)(2,1)S(1)}, u32[]{:S(2)}, u32[]{:S(2)}) %all-to-all-start) | async-done | bytes 196640 | tf_op jit(solution)/shard_map/all_to_all | solution.py:105
  53.0 5.4 %all-to-all-start.2 = ((bf16[16,2,3072]{2,1,0:T(2,128)(2,1)}), bf16[16,2,3072]{2,1,0:T(2,128)(2,1)S(1)}, u32[]{:S(2)}, u32[]{:S(2)}) async-start(bf16[16,2,3072]{2,1,0:T(2,128)(2,1)} %reshape.350), calls=%async_computation.2 | async-start | bytes 393216 | tf_op jit(solution)/shard_map/all_to_all | solution.py:106
  59.3 1.1 reduce.6
  61.3 1.1 reduce.3
  63.2 2.5 all-to-all-done.2
  65.8 1.1 reduce.7
  67.7 2.7 %while.13 = (s32[]{:T(128)}, f32[2,768,64]{1,2,0:T(8,128)S(1)}, f32[2,768]{1,0:T(2,128)S(1)}, pred[3,256]{1,0:T(4,128)(4,1)S(1)}, bf16[3,256,2,64]{1,3,2,0:T(8,1...) while((s32[]{:T(128)}, f32[2,768,64]{1,2,0:T(8,128)S(1)}, ...), condition=%wide.region_6.7_spmd.clone, body=%wide.region_4.6_spmd.clone.sunk | while | flops 102434304 | bytes 2712692 | solution.py:142
  71.8 1.7 reduce.25
  74.3 5.2 %all-to-all-start.3 = ((bf16[16,2,3072]{2,1,0:T(2,128)(2,1)}), bf16[16,2,3072]{2,1,0:T(2,128)(2,1)S(1)}, u32[]{:S(2)}, u32[]{:S(2)}) async-start(bf16[16,2,3072]{2,1,0:T(2,128)(2,1)} %reshape.352), calls=%async_computation.3 | async-start | bytes 393216 | tf_op jit(solution)/shard_map/all_to_all | solution.py:146
  80.3 9.6 %all-to-all-done.3 = bf16[16,2,3072]{2,1,0:T(2,128)(2,1)S(1)} async-done(((bf16[16,2,3072]{2,1,0:T(2,128)(2,1)}), bf16[16,2,3072]{2,1,0:T(2,128)(2,1)S(1)}, u32[]{:S(2)}, u32[]{:S(2)}) %all-to-all-start.3) | async-done | bytes 196640 | tf_op jit(solution)/shard_map/all_to_all | solution.py:146
  90.0 1.1 reduce.8
  92.2 2.8 %fusion.29 = f32[1,3072]{1,0:T(1,128)S(1)} fusion(bf16[512,1]{0,1:T(2,128)(2,1)S(1)} %reshape.315, bf16[512,3072]{0,1:T(8,128)(2,1)} %all-gather.4.cloned.1.call-done), kind=kOutput, calls=%fused_computation.82 | convolution fusion | flops 3145728 | bytes 3159040 | tf_op jit(solution)/shard_map/dot_general | solution.py:154
  95.0 34.2 %all-gather.8.cloned.1.call-done = bf16[512,6144]{1,0:T(8,128)(2,1)} async-done(((bf16[512,384]{1,0:T(8,128)(2,1)}), bf16[512,6144]{1,0:T(8,128)(2,1)}) %all-gather.8.cloned.1.call-update) | async-done | bytes 6291472 | tf_op jit(solution)/shard_map/all_gather | solution.py:152
  129.1 3.7 %fusion.30 = f32[1,6144]{1,0:T(1,128)S(1)} fusion(bf16[512,1]{0,1:T(2,128)(2,1)S(1)} %reshape.315, bf16[512,6144]{1,0:T(8,128)(2,1)} %all-gather.8.cloned.1.call-done), kind=kOutput, calls=%fused_computation.83 | convolution fusion | flops 6291456 | bytes 6317056 | tf_op jit(solution)/shard_map/dot_general | solution.py:155
  132.8 93.4 %all-gather.6.cloned.1.call-done = bf16[2048,3072]{0,1:T(8,128)(2,1)} async-done(((bf16[2048,96]{0,1:T(8,128)(2,1)}), bf16[2048,3072]{0,1:T(8,128)(2,1)}) %all-gather.6.cloned.1.call-update) | async-done | bytes 12582928 | tf_op jit(solution)/shard_map/all_gather | solution.py:158
  226.2 8.6 %fusion.27 = (f32[48]{0:T(128)S(1)}, f32[48,3072]{1,0:T(8,128)S(1)}) fusion(bf16[48,2048]{1,0:T(8,128)(2,1)S(1)} %reshape.307, bf16[2048,3072]{0,1:T(8,128)(2,1)} %all-gather.6.cloned.1.call-done, f32[3072]{0:T(1024)S(1)} %bitcast.126, bf16[1,48,3072]{2,1,0:T(8,128)(2,1)S(1)} %copy-done.1), kind=kOutput, calls=%fused_computation.80 | convolution fusion | flops 604569536 | bytes 13676736 | tf_op jit(solution)/shard_map/dot_general | solution.py:156
  236.4 1.8 collective-permute-done
  238.2 1.4 add_select_fusion
  (133 shorter events, 18.9 us)
Async XLA Ops:
  6.5 228.5 %copy-start = (bf16[3072,64]{0,1:T(8,128)(2,1)S(1)}, bf16[3072,64]{0,1:T(8,128)(2,1)}, u32[]{:S(2)}) copy-start(bf16[3072,64]{0,1:T(8,128)(2,1)} %param.33) | copy-start | bytes 1179652
  6.5 3.5 %copy-start.15 = (f32[2,64]{1,0:T(2,128)S(1)}, f32[2,64]{1,0:T(2,128)}, u32[]{:S(2)}) copy-start(f32[2,64]{1,0:T(2,128)} %param.25) | copy-start | bytes 1540
  6.5 3.6 %copy-start.14 = (f32[2,64]{1,0:T(2,128)S(1)}, f32[2,64]{1,0:T(2,128)}, u32[]{:S(2)}) copy-start(f32[2,64]{1,0:T(2,128)} %param.26) | copy-start | bytes 1540
  6.5 4.4 %copy-start.3 = (bf16[1,48,2048]{2,1,0:T(8,128)(2,1)S(1)}, bf16[1,48,2048]{2,1,0:T(8,128)(2,1)}, u32[]{:S(2)}) copy-start(bf16[1,48,2048]{2,1,0:T(8,128)(2,1)} %param.22) | copy-start | bytes 589828
  6.5 85.6 %all-gather.4.cloned.1.call-start = ((), (), s32[]{:S(2)}) async-start(), calls=%async_computation.4 | async-start | bytes 3342336 | tf_op jit(solution)/shard_map/all_gather | solution.py:151
  7.3 121.9 %all-gather.8.cloned.1.call-start = ((), (), s32[]{:S(2)}) async-start(), calls=%async_computation.6 | async-start | bytes 6684672 | tf_op jit(solution)/shard_map/all_gather | solution.py:152
  8.0 218.2 %all-gather.6.cloned.1.call-start = ((), (), s32[]{:S(2)}) async-start(), calls=%async_computation.5 | async-start | bytes 12976128 | tf_op jit(solution)/shard_map/all_gather | solution.py:158
  10.0 1.8 copy-start.11
  10.0 1.8 copy-start.20
  10.0 1.9 copy-start.19
  11.8 7.3 %copy-start.7 = (pred[48]{0:T(512)(128)(4,1)}, pred[48]{0:T(512)(128)(4,1)S(1)}, u32[]{:S(2)}) copy-start(pred[48]{0:T(512)(128)(4,1)S(1)} %add_compare_fusion) | copy-start | bytes 148
  12.5 1.7 copy-start.4
  14.1 4.9 %copy-start.9 = (f32[64]{0:T(128)S(1)}, f32[64]{0:T(128)}, u32[]{:S(2)}) copy-start(f32[64]{0:T(128)} %get-tuple-element.119) | copy-start | bytes 772
  14.1 4.9 %copy-start.10 = (f32[64]{0:T(128)S(1)}, f32[64]{0:T(128)}, u32[]{:S(2)}) copy-start(f32[64]{0:T(128)} %get-tuple-element.127) | copy-start | bytes 772
  19.4 12.8 %copy-start.18 = (f32[64]{0:T(128)S(1)}, f32[64]{0:T(128)}, u32[]{:S(2)}) copy-start(f32[64]{0:T(128)} %get-tuple-element.121) | copy-start | bytes 772
  19.4 12.9 %copy-start.17 = (f32[64]{0:T(128)S(1)}, f32[64]{0:T(128)}, u32[]{:S(2)}) copy-start(f32[64]{0:T(128)} %get-tuple-element.126) | copy-start | bytes 772
  19.5 12.9 %copy-start.5 = (f32[48,32]{0,1:T(8,128)S(1)}, f32[48,32]{0,1:T(8,128)}, u32[]{:S(2)}) copy-start(f32[48,32]{0,1:T(8,128)} %copy-done.4) | copy-start | bytes 18436
  19.9 12.7 %copy-start.8 = (pred[48]{0:T(512)(128)(4,1)S(1)}, pred[48]{0:T(512)(128)(4,1)}, u32[]{:S(2)}) copy-start(pred[48]{0:T(512)(128)(4,1)} %copy-done.7) | copy-start | bytes 148
  23.1 13.9 %all-to-all-start.1 = ((bf16[16,2,3072]{2,1,0:T(2,128)(2,1)}), bf16[16,2,3072]{2,1,0:T(2,128)(2,1)S(1)}, u32[]{:S(2)}, u32[]{:S(2)}) async-start(bf16[16,2,3072]{2,1,0:T(2,128)(2,1)} %reshape.348), calls=%async_computation.1 | async-start | bytes 393216 | tf_op jit(solution)/shard_map/all_to_all | solution.py:104
  32.6 9.6 %copy-start.2 = (bf16[1,48,2048]{2,1,0:T(8,128)(2,1)S(1)}, bf16[1,48,2048]{2,1,0:T(8,128)(2,1)}, u32[]{:S(2)}) copy-start(bf16[1,48,2048]{2,1,0:T(8,128)(2,1)} %param.24) | copy-start | bytes 589828
  37.0 16.0 %all-to-all-start = ((bf16[16,2,3072]{2,1,0:T(2,128)(2,1)}), bf16[16,2,3072]{2,1,0:T(2,128)(2,1)S(1)}, u32[]{:S(2)}, u32[]{:S(2)}) async-start(bf16[16,2,3072]{2,1,0:T(2,128)(2,1)} %reshape.346), calls=%async_computation | async-start | bytes 393216 | tf_op jit(solution)/shard_map/all_to_all | solution.py:105
  53.0 12.6 %all-to-all-start.2 = ((bf16[16,2,3072]{2,1,0:T(2,128)(2,1)}), bf16[16,2,3072]{2,1,0:T(2,128)(2,1)S(1)}, u32[]{:S(2)}, u32[]{:S(2)}) async-start(bf16[16,2,3072]{2,1,0:T(2,128)(2,1)} %reshape.350), calls=%async_computation.2 | async-start | bytes 393216 | tf_op jit(solution)/shard_map/all_to_all | solution.py:106
  70.3 9.2 %copy-start.12 = (bf16[512]{0:T(512)(128)(2,1)S(1)}, bf16[512]{0:T(512)(128)(2,1)}, u32[]{:S(2)}) copy-start(bf16[512]{0:T(512)(128)(2,1)} %param.29) | copy-start | bytes 3076
  70.3 9.9 %copy-start.13 = (f32[2,50]{1,0:T(2,128)S(1)}, f32[2,50]{1,0:T(2,128)}, u32[]{:S(2)}) copy-start(f32[2,50]{1,0:T(2,128)} %param.36) | copy-start | bytes 1204
  74.3 15.6 %all-to-all-start.3 = ((bf16[16,2,3072]{2,1,0:T(2,128)(2,1)}), bf16[16,2,3072]{2,1,0:T(2,128)(2,1)S(1)}, u32[]{:S(2)}, u32[]{:S(2)}) async-start(bf16[16,2,3072]{2,1,0:T(2,128)(2,1)} %reshape.352), calls=%async_computation.3 | async-start | bytes 393216 | tf_op jit(solution)/shard_map/all_to_all | solution.py:146
  95.0 131.2 %copy-start.1 = (bf16[1,48,3072]{2,1,0:T(8,128)(2,1)S(1)}, bf16[1,48,3072]{2,1,0:T(8,128)(2,1)}, u32[]{:S(2)}) copy-start(bf16[1,48,3072]{2,1,0:T(8,128)(2,1)} %param.21) | copy-start | bytes 884740
  226.2 8.8 %copy-start.16 = (f32[64]{0:T(128)S(1)}, f32[64]{0:T(128)}, u32[]{:S(2)}) copy-start(f32[64]{0:T(128)} %param.34) | copy-start | bytes 772
  226.2 12.0 %copy-start.6 = (f32[48,64]{1,0:T(8,128)S(1)}, f32[48,64]{1,0:T(8,128)}, u32[]{:S(2)}) copy-start(f32[48,64]{1,0:T(8,128)} %param.35) | copy-start | bytes 36868
  235.5 2.7 %collective-permute-start = (f32[48,32]{1,0:T(8,128)S(1)}, f32[48,32]{1,0:T(8,128)S(1)}, u32[]{:S(2)}, u32[]{:S(2)}) collective-permute-start(f32[48,32]{1,0:T(8,128)S(1)} %constant_dynamic-slice_fusion), channel_id=1, source_target_pairs={{0,16},{16,0},{1,17},{17,1},{2,18},{18,2},{3,19},{19,3},{4,20},{20... | collective-permute-start | bytes 18440 | tf_op jit(solution)/shard_map/ppermute | solution.py:16
Sparse Core Ops, SparseCore 0:
  9.7 49.2 all-gather.3
  61.2 67.9 all-gather.7
  132.0 94.1 all-gather.5
where the time goes:
time: 250 us; the launch traced here: 247 us
  waiting for transfers between devices  153 us (61%)
  other arithmetic  23.7 us (9%)
  starting transfers between devices  23 us (9%)
  matrix products  17.8 us (7%)
  between operations  15.2 us (6%)
  local copies, waits for them, and re-layouts  14.4 us (6%)
    all_gather x1, waiting for transfers between devices, on_device(): lax.all_gather(out_weight, ('cfg', 'seq'), axis=1, tiled=True)  93.4 us
    all_gather x1, waiting for transfers between devices, on_device(): lax.all_gather(mod_table, 'seq', axis=1, tiled=True)  34.2 us
    all_to_all x1, waiting for transfers between devices, on_device(): lax.all_to_all(back_send, 'seq', split_axis=0, concat_axis=0, tiled=True)  9.59 us
    dot_general x1, matrix products, on_device(): jnp.dot(attended_rows, lax.all_gather(out_weight, ('cfg', 'seq'), axis=1,...  8.56 us
    all_to_all x1, waiting for transfers between devices, on_device(): lax.all_to_all(key_send, 'seq', split_axis=0, concat_axis=0, tiled=True)  8.14 us
    all_to_all x1, starting transfers between devices, on_device(): lax.all_to_all(query_send, 'seq', split_axis=0, concat_axis=0, tiled=True)  6.67 us
    unnamed x56, local copies, waits for them, and re-layouts  6.53 us
    all_to_all x1, starting transfers between devices, on_device(): lax.all_to_all(value_send, 'seq', split_axis=0, concat_axis=0, tiled=True)  5.45 us
  transfers between devices with their start and end apart: 8, of which 7 were waited for; matrix products, arithmetic and copies ran while one was open for 18% of the time, Pallas kernels for 0%

commit v1 on v0

--- a/solution.py
+++ b/solution.py
@@ -54,6 +54,40 @@
         axis=-1,
     ).reshape(row_count, head_count, 64)
     return jnp.where(is_video[:, None, None], rotated, normed).astype(jnp.bfloat16)
+
+
+def project_columns(attended, out_weight, seq_count, local_rows):
+    head_group, query_count, _ = attended.shape
+    own_width = out_weight.shape[1]
+    partner_weight = swapped(out_weight, "cfg", 0)
+    cfg_place = lax.axis_index("cfg")
+    is_first = cfg_place == 0
+    first = jnp.where(is_first, out_weight, partner_weight)
+    second = jnp.where(is_first, partner_weight, out_weight)
+    weights = jnp.concatenate([first, second], axis=1)
+    own_heads = attended.transpose(1, 0, 2).reshape(query_count, head_group * 64)
+    every = lax.all_gather(own_heads, "seq", axis=0)
+    weights = weights.reshape(seq_count, head_group * 64, 2 * own_width)
+    part = jnp.einsum("sqk,skn->qn", every, weights, preferred_element_type=jnp.float32)
+    sent = part.astype(jnp.bfloat16).reshape(seq_count, local_rows * 2 * own_width)
+    back = lax.all_to_all(sent, "seq", split_axis=0, concat_axis=0, tiled=True)
+    back = back.reshape(seq_count, local_rows, 2, own_width).transpose(1, 2, 0, 3)
+    return back.reshape(local_rows, 2 * seq_count * own_width).astype(jnp.float32)
+
+
+def project_rows(attended, out_weight, seq_count, part_rows, row_split, head_sets):
+    head_group = attended.shape[0]
+    back_send = attended.reshape(head_group, seq_count, part_rows, 64).transpose(1, 2, 0, 3)
+    back_send = back_send.reshape(seq_count, part_rows * head_group * 64)
+    back_recv = lax.all_to_all(back_send, "seq", split_axis=0, concat_axis=0, tiled=True)
+    attended_rows = back_recv.reshape(head_sets, row_split, part_rows, head_group, 64)
+    attended_rows = attended_rows.transpose(1, 2, 0, 3, 4)
+    attended_rows = attended_rows.reshape(row_split * part_rows, head_sets * head_group * 64)
+    return jnp.dot(
+        attended_rows,
+        lax.all_gather(out_weight, ("cfg", "seq"), axis=1, tiled=True),
+        preferred_element_type=jnp.float32,
+    )
 
 
 def on_device(
@@ -141,23 +175,17 @@
     )
     final_state, unused_out = lax.scan(key_step, start_state, scanned)
     attended = (final_state[0] / final_state[1][..., None]).astype(jnp.bfloat16)
-    back_send = attended.reshape(head_group, seq_count, part_rows, 64).transpose(1, 2, 0, 3)
-    back_send = back_send.reshape(seq_count, part_rows * head_group * 64)
-    back_recv = lax.all_to_all(back_send, "seq", split_axis=0, concat_axis=0, tiled=True)
-    attended_rows = back_recv.reshape(head_sets, row_split, part_rows, head_group, 64)
-    attended_rows = attended_rows.transpose(1, 2, 0, 3, 4).reshape(local_rows, head_count * 64)
     embed_act = jax.nn.silu(time_embed.astype(jnp.float32)).astype(jnp.bfloat16)[None, :]
-    gate_full, mod_full = (
-        lax.all_gather(gate_table, "seq", axis=1, tiled=True),
-        lax.all_gather(mod_table, "seq", axis=1, tiled=True),
-    )
-    gate_vec = jnp.dot(embed_act, gate_full, preferred_element_type=jnp.float32)[0]
-    modulation = jnp.dot(embed_act, mod_full, preferred_element_type=jnp.float32)[0]
-    projected = jnp.dot(
-        attended_rows,
-        lax.all_gather(out_weight, ("cfg", "seq"), axis=1, tiled=True),
-        preferred_element_type=jnp.float32,
-    )
+    gate_own = jnp.dot(embed_act, gate_table, preferred_element_type=jnp.float32)
+    mod_own = jnp.dot(embed_act, mod_table, preferred_element_type=jnp.float32)
+    gate_width = gate_own.shape[1]
+    vectors = lax.all_gather(jnp.concatenate([gate_own, mod_own], axis=1)[0], "seq", axis=0)
+    gate_vec = vectors[:, :gate_width].reshape(-1)
+    modulation = vectors[:, gate_width:].reshape(-1)
+    if row_split == 1:
+        projected = project_columns(attended, out_weight, seq_count, local_rows)
+    else:
+        projected = project_rows(attended, out_weight, seq_count, part_rows, row_split, head_sets)
     model_width = hidden.shape[2]
     residual = hidden[0].astype(jnp.float32) + gate_vec[None, :] * projected
     normed = (

time: 250 us -> 164 us (0.66)
  the two profiles are of different devices: /device:TPU:3 before, /device:TPU:0 now
where the time goes in v1:
time: 164 us; the launch traced here: 163 us
  waiting for transfers between devices  57.6 us (35%)
  other arithmetic  24.3 us (15%)
  blocking collectives  22.2 us (14%)
  starting transfers between devices  21.3 us (13%)
  local copies, waits for them, and re-layouts  16.2 us (10%)
  between operations  15.6 us (10%)
  matrix products  6.13 us (4%)
    all_gather x1, waiting for transfers between devices, project_columns(): every = lax.all_gather(own_heads, 'seq', axis=0)  33.1 us
    all_gather x1, blocking collectives, on_device(): lax.all_gather(jnp.concatenate([gate_own, mod_own], axis=1)[0], 'seq', ax...  22.2 us
    ppermute x2, waiting for transfers between devices, swapped(): lax.ppermute(value, axis, [(i, i ^ 1 << bit) for i in range(lax.axis_size...  10.4 us
    all_to_all x1, starting transfers between devices, on_device(): lax.all_to_all(query_send, 'seq', split_axis=0, concat_axis=0, tiled=True)  7.36 us
    unnamed x75, local copies, waits for them, and re-layouts  7.16 us
    all_to_all x1, waiting for transfers between devices, on_device(): lax.all_to_all(key_send, 'seq', split_axis=0, concat_axis=0, tiled=True)  6.22 us
    all_to_all x1, waiting for transfers between devices, on_device(): lax.all_to_all(value_send, 'seq', split_axis=0, concat_axis=0, tiled=True)  3.97 us
    all_to_all x1, waiting for transfers between devices, on_device(): lax.all_to_all(query_send, 'seq', split_axis=0, concat_axis=0, tiled=True)  3.9 us
  transfers between devices with their start and end apart: 7, of which 6 were waited for; matrix products, arithmetic and copies ran while one was open for 8% of the time, Pallas kernels for 0%

profile of v1, /device:TPU:0, one launch (start us, length us, event | category | flops | bytes accessed | tf_op | source)
XLA Modules:
  0.0 163.4 jit_solution(8436904069699191732)
XLA Ops:
  6.5 1.2 copy.51
  12.2 3.4 %multiply_subtract_fusion = (bf16[48,32,32,1]{0,3,2,1:T(2,128)(2,1)S(1)}, bf16[48,32,32,1]{0,3,2,1:T(2,128)(2,1)S(1)}, bf16[48,32,32,1]{0,3,2,1:T(2,128)(2,1)S(1)}, bf16[48,32,32,1]{0,3,2,1:T(2,128)(2,1)}) fusion(f32[48,32,32,2]{0,3,2,1:T(2,128)S(1)} %multiply_add_fusion, f32[48,32]{0,1:T(8,128)S(1)} %get-tuple-element.121, ...), kind=kLoop, calls=%fused_computation.38 | loop fusion | flops 786432 | bytes 1191936 | tf_op jit(solution)/shard_map/sub | solution.py:53
  15.7 1.4 pad_maximum_fusion.1
  18.7 1.7 %reduce.24 = bf16[16,6144]{1,0:T(8,128)(2,1)S(1)} reduce(bf16[16,1,6144]{2,1,0:T(2,128)(2,1)S(1)} %all_to_all.33, bf16[]{:T(256)} %broadcast.256), dimensions={1}, to_apply=%all_to_all.33.reduce_sub_computation | reduce | bytes 393218 | tf_op jit(solution)/shard_map/all_to_all | solution.py:138
  21.2 7.4 %all-to-all-start.1 = ((bf16[16,2,3072]{2,1,0:T(2,128)(2,1)}), bf16[16,2,3072]{2,1,0:T(2,128)(2,1)S(1)}, u32[]{:S(2)}, u32[]{:S(2)}) async-start(bf16[16,2,3072]{2,1,0:T(2,128)(2,1)} %reshape.358), calls=%async_computation.1 | async-start | bytes 393216 | tf_op jit(solution)/shard_map/all_to_all | solution.py:138
  28.6 1.4 pad_maximum_fusion
  31.1 1.7 %reduce.23 = bf16[16,6144]{1,0:T(8,128)(2,1)S(1)} reduce(bf16[16,1,6144]{2,1,0:T(2,128)(2,1)S(1)} %all_to_all.32, bf16[]{:T(256)} %broadcast.256), dimensions={1}, to_apply=%all_to_all.32.reduce_sub_computation | reduce | bytes 393218 | tf_op jit(solution)/shard_map/all_to_all | solution.py:139
  32.9 0.8 reshape.356
  33.7 3.9 %all-to-all-done.1 = bf16[16,2,3072]{2,1,0:T(2,128)(2,1)S(1)} async-done(((bf16[16,2,3072]{2,1,0:T(2,128)(2,1)}), bf16[16,2,3072]{2,1,0:T(2,128)(2,1)S(1)}, u32[]{:S(2)}, u32[]{:S(2)}) %all-to-all-start.1) | async-done | bytes 196640 | tf_op jit(solution)/shard_map/all_to_all | solution.py:138
  37.6 3.5 %all-to-all-start = ((bf16[16,2,3072]{2,1,0:T(2,128)(2,1)}), bf16[16,2,3072]{2,1,0:T(2,128)(2,1)S(1)}, u32[]{:S(2)}, u32[]{:S(2)}) async-start(bf16[16,2,3072]{2,1,0:T(2,128)(2,1)} %reshape.356), calls=%async_computation | async-start | bytes 393216 | tf_op jit(solution)/shard_map/all_to_all | solution.py:139
  41.3 1.7 %reduce.25 = bf16[16,6144]{1,0:T(8,128)(2,1)S(1)} reduce(bf16[16,1,6144]{2,1,0:T(2,128)(2,1)S(1)} %all_to_all.34, bf16[]{:T(256)} %broadcast.256), dimensions={1}, to_apply=%all_to_all.34.reduce_sub_computation | reduce | bytes 393218 | tf_op jit(solution)/shard_map/all_to_all | solution.py:140
  43.9 6.2 %all-to-all-done = bf16[16,2,3072]{2,1,0:T(2,128)(2,1)S(1)} async-done(((bf16[16,2,3072]{2,1,0:T(2,128)(2,1)}), bf16[16,2,3072]{2,1,0:T(2,128)(2,1)S(1)}, u32[]{:S(2)}, u32[]{:S(2)}) %all-to-all-start) | async-done | bytes 196640 | tf_op jit(solution)/shard_map/all_to_all | solution.py:139
  50.1 3.5 %all-to-all-start.2 = ((bf16[16,2,3072]{2,1,0:T(2,128)(2,1)}), bf16[16,2,3072]{2,1,0:T(2,128)(2,1)S(1)}, u32[]{:S(2)}, u32[]{:S(2)}) async-start(bf16[16,2,3072]{2,1,0:T(2,128)(2,1)} %reshape.360), calls=%async_computation.2 | async-start | bytes 393216 | tf_op jit(solution)/shard_map/all_to_all | solution.py:140
  54.7 1.1 reduce.6
  56.7 1.1 reduce.3
  58.6 4.0 %all-to-all-done.2 = bf16[16,2,3072]{2,1,0:T(2,128)(2,1)S(1)} async-done(((bf16[16,2,3072]{2,1,0:T(2,128)(2,1)}), bf16[16,2,3072]{2,1,0:T(2,128)(2,1)S(1)}, u32[]{:S(2)}, u32[]{:S(2)}) %all-to-all-start.2) | async-done | bytes 196640 | tf_op jit(solution)/shard_map/all_to_all | solution.py:140
  62.7 1.1 reduce.7
  64.6 2.7 %while.13 = (s32[]{:T(128)}, f32[2,768,64]{1,2,0:T(8,128)S(1)}, f32[2,768]{1,0:T(2,128)S(1)}, pred[3,256]{1,0:T(4,128)(4,1)S(1)}, bf16[3,256,2,64]{1,3,2,0:T(8,1...) while((s32[]{:T(128)}, f32[2,768,64]{1,2,0:T(8,128)S(1)}, ...), condition=%wide.region_6.7_spmd.clone, body=%wide.region_4.6_spmd.clone.sunk | while | flops 102434304 | bytes 2712692 | solution.py:176
  67.3 0.8 copy.62
  68.2 1.6 collective-permute-start
  70.0 8.6 %collective-permute-done = bf16[2048,96]{0,1:T(8,128)(2,1)S(1)} collective-permute-done((bf16[2048,96]{0,1:T(8,128)(2,1)S(1)}, bf16[2048,96]{0,1:T(8,128)(2,1)S(1)}, u32[]{:S(2)}, u32[]{:S(2)}) %collective-permute-start) | collective-permute-done | bytes 393248 | tf_op jit(solution)/shard_map/ppermute | solution.py:16
  78.7 33.1 %all-gather.3.cloned.1.call-done = bf16[16,768,128]{2,1,0:T(8,128)(2,1)} async-done(((bf16[1,768,128]{2,1,0:T(8,128)(2,1)}), bf16[16,768,128]{2,1,0:T(8,128)(2,1)}) %all-gather.3.cloned.1.call-update) | async-done | bytes 3145744 | tf_op jit(solution)/shard_map/all_gather | solution.py:69
  111.7 3.1 %fusion.6 = bf16[768,192]{0,1:T(8,128)(2,1)S(1)} fusion(bf16[16,768,128]{2,1,0:T(8,128)(2,1)} %all-gather.3.cloned.1.call-done, bf16[2048,96]{0,1:T(8,128)(2,1)S(1)} %get-tuple-element.115, bf16[2048,96]{0,1:T(8,128)(2,1)S(1)} %get-tuple-element.114), kind=kOutput, calls=%fused_computation.13 | convolution fusion | flops 605700096 | bytes 4227072 | tf_op jit(solution)/shard_map/sqk,skn->qn/dot_general | solution.py:71
  115.6 2.4 %reduce.26 = bf16[16,9216]{1,0:T(8,128)(2,1)S(1)} reduce(bf16[16,1,9216]{2,1,0:T(2,128)(2,1)S(1)} %all_to_all.35, bf16[]{:T(256)} %broadcast.256), dimensions={1}, to_apply=%all_to_all.35.reduce_sub_computation | reduce | bytes 589826 | tf_op jit(solution)/shard_map/all_to_all | solution.py:73
  117.9 0.9 reshape.362
  118.9 3.5 %all-to-all-start.3 = ((bf16[16,2,4608]{2,1,0:T(2,128)(2,1)}), bf16[16,2,4608]{2,1,0:T(2,128)(2,1)S(1)}, u32[]{:S(2)}, u32[]{:S(2)}) async-start(bf16[16,2,4608]{2,1,0:T(2,128)(2,1)} %reshape.362), calls=%async_computation.3 | async-start | bytes 589824 | tf_op jit(solution)/shard_map/all_to_all | solution.py:73
  122.6 22.2 %all-gather = f32[16,1,576]{2,1,0:T(1,128)S(1)} all-gather(f32[1,1,576]{2,1,0:T(1,128)S(1)} %maximum_bitcast_fusion.1), channel_id=1, replica_groups=mesh['cfg'=2,'seq'=16] {'seq'}, dimensions={0}, use_global_device_ids=true | all-gather | bytes 39168 | tf_op jit(solution)/shard_map/all_gather | solution.py:182
  146.0 1.6 %convert_reduce_fusion = f32[16,9216]{1,0:T(8,128)S(1)} fusion(bf16[16,1,9216]{2,1,0:T(2,128)(2,1)S(1)} %reshape.363), kind=kLoop, calls=%fused_computation.32 | loop fusion | flops 147456 | bytes 884736 | tf_op jit(solution)/shard_map/convert_element_type | solution.py:75
  147.6 1.1 reshape.320
  150.6 1.5 collective-permute-start.1
  152.7 1.8 %collective-permute-done.1 = f32[48,32]{1,0:T(8,128)S(1)} collective-permute-done((f32[48,32]{1,0:T(8,128)S(1)}, f32[48,32]{1,0:T(8,128)S(1)}, u32[]{:S(2)}, u32[]{:S(2)}) %collective-permute-start.1) | collective-permute-done | bytes 6176 | tf_op jit(solution)/shard_map/ppermute | solution.py:16
  154.4 1.4 add_select_fusion
  (156 shorter events, 18.8 us)
Async XLA Ops:
  6.5 143.6 %copy-start = (bf16[3072,64]{0,1:T(8,128)(2,1)S(1)}, bf16[3072,64]{0,1:T(8,128)(2,1)}, u32[]{:S(2)}) copy-start(bf16[3072,64]{0,1:T(8,128)(2,1)} %param.33) | copy-start | bytes 1179652
  7.8 1.5 copy-start.9
  8.5 2.1 %copy-start.10 = (f32[48,32]{0,1:T(8,128)}, f32[48,32]{0,1:T(8,128)S(1)}, u32[]{:S(2)}) copy-start(f32[48,32]{0,1:T(8,128)S(1)} %add_rsqrt_fusion.1) | copy-start | bytes 18436
  9.8 1.6 copy-start.5
  10.0 2.2 %copy-start.12 = (f32[48,32]{0,1:T(8,128)}, f32[48,32]{0,1:T(8,128)S(1)}, u32[]{:S(2)}) copy-start(f32[48,32]{0,1:T(8,128)S(1)} %add_rsqrt_fusion) | copy-start | bytes 18436
  10.3 6.8 %copy-start.15 = (pred[48]{0:T(512)(128)(4,1)}, pred[48]{0:T(512)(128)(4,1)S(1)}, u32[]{:S(2)}) copy-start(pred[48]{0:T(512)(128)(4,1)S(1)} %add_compare_fusion) | copy-start | bytes 148
  15.7 1.4 copy-start.6
  15.7 1.4 copy-start.13
  15.7 1.4 copy-start.18
  15.7 1.4 copy-start.19
  17.5 11.1 %copy-start.1 = (bf16[48,32,32,1]{0,3,2,1:T(2,128)(2,1)S(1)}, bf16[48,32,32,1]{0,3,2,1:T(2,128)(2,1)}, u32[]{:S(2)}) copy-start(bf16[48,32,32,1]{0,3,2,1:T(2,128)(2,1)} %get-tuple-element.119) | copy-start | bytes 294916
  18.1 11.9 %copy-start.26 = (f32[64]{0:T(128)S(1)}, f32[64]{0:T(128)}, u32[]{:S(2)}) copy-start(f32[64]{0:T(128)} %get-tuple-element.130) | copy-start | bytes 772
  18.1 12.0 %copy-start.25 = (f32[64]{0:T(128)S(1)}, f32[64]{0:T(128)}, u32[]{:S(2)}) copy-start(f32[64]{0:T(128)} %get-tuple-element.133) | copy-start | bytes 772
  18.1 12.1 %copy-start.11 = (f32[48,32]{0,1:T(8,128)S(1)}, f32[48,32]{0,1:T(8,128)}, u32[]{:S(2)}) copy-start(f32[48,32]{0,1:T(8,128)} %copy-done.10) | copy-start | bytes 18436
  21.2 16.4 %all-to-all-start.1 = ((bf16[16,2,3072]{2,1,0:T(2,128)(2,1)}), bf16[16,2,3072]{2,1,0:T(2,128)(2,1)S(1)}, u32[]{:S(2)}, u32[]{:S(2)}) async-start(bf16[16,2,3072]{2,1,0:T(2,128)(2,1)} %reshape.358), calls=%async_computation.1 | async-start | bytes 393216 | tf_op jit(solution)/shard_map/all_to_all | solution.py:138
  28.6 1.7 %copy-start.16 = (pred[48]{0:T(512)(128)(4,1)S(1)}, pred[48]{0:T(512)(128)(4,1)}, u32[]{:S(2)}) copy-start(pred[48]{0:T(512)(128)(4,1)} %copy-done.15) | copy-start | bytes 148
  30.8 10.3 %copy-start.7 = (bf16[1,48,2048]{2,1,0:T(8,128)(2,1)S(1)}, bf16[1,48,2048]{2,1,0:T(8,128)(2,1)}, u32[]{:S(2)}) copy-start(bf16[1,48,2048]{2,1,0:T(8,128)(2,1)} %param.24) | copy-start | bytes 589828
  37.6 12.5 %all-to-all-start = ((bf16[16,2,3072]{2,1,0:T(2,128)(2,1)}), bf16[16,2,3072]{2,1,0:T(2,128)(2,1)S(1)}, u32[]{:S(2)}, u32[]{:S(2)}) async-start(bf16[16,2,3072]{2,1,0:T(2,128)(2,1)} %reshape.356), calls=%async_computation | async-start | bytes 393216 | tf_op jit(solution)/shard_map/all_to_all | solution.py:139
  50.1 12.5 %all-to-all-start.2 = ((bf16[16,2,3072]{2,1,0:T(2,128)(2,1)}), bf16[16,2,3072]{2,1,0:T(2,128)(2,1)S(1)}, u32[]{:S(2)}, u32[]{:S(2)}) async-start(bf16[16,2,3072]{2,1,0:T(2,128)(2,1)} %reshape.360), calls=%async_computation.2 | async-start | bytes 393216 | tf_op jit(solution)/shard_map/all_to_all | solution.py:140
  53.6 58.1 %all-gather.3.cloned.1.call-start = ((), (), s32[]{:S(2)}) async-start(), calls=%async_computation.4 | async-start | bytes 3342336 | tf_op jit(solution)/shard_map/all_gather | solution.py:69
  64.6 3.6 %copy-start.4 = (bf16[2048,96]{0,1:T(8,128)(2,1)S(1)}, bf16[2048,96]{0,1:T(8,128)(2,1)}, u32[]{:S(2)}) copy-start(bf16[2048,96]{0,1:T(8,128)(2,1)} %param.32) | copy-start | bytes 1179652
  64.6 5.2 %copy-start.21 = (bf16[512]{0:T(512)(128)(2,1)S(1)}, bf16[512]{0:T(512)(128)(2,1)}, u32[]{:S(2)}) copy-start(bf16[512]{0:T(512)(128)(2,1)} %param.29) | copy-start | bytes 3076
  64.6 5.2 %copy-start.3 = (bf16[512,384]{1,0:T(8,128)(2,1)S(1)}, bf16[512,384]{1,0:T(8,128)(2,1)}, u32[]{:S(2)}) copy-start(bf16[512,384]{1,0:T(8,128)(2,1)} %param.31) | copy-start | bytes 1179652
  68.2 10.4 %collective-permute-start = (bf16[2048,96]{0,1:T(8,128)(2,1)S(1)}, bf16[2048,96]{0,1:T(8,128)(2,1)S(1)}, u32[]{:S(2)}, u32[]{:S(2)}) collective-permute-start(bf16[2048,96]{0,1:T(8,128)(2,1)S(1)} %copy-done.4), channel_id=1, source_target_pairs={{0,16},{16,0},{1,17},{17,1},{2,18},{18,2},{3,19},{19,3},{4,20},{20... | collective-permute-start | bytes 1179656 | tf_op jit(solution)/shard_map/ppermute | solution.py:16
  115.0 7.4 %copy-start.8 = (bf16[512,192]{0,1:T(8,128)(2,1)S(1)}, bf16[512,192]{0,1:T(8,128)(2,1)}, u32[]{:S(2)}) copy-start(bf16[512,192]{0,1:T(8,128)(2,1)} %param.30) | copy-start | bytes 589828
  115.0 30.6 %copy-start.22 = (f32[2,50]{1,0:T(2,128)S(1)}, f32[2,50]{1,0:T(2,128)}, u32[]{:S(2)}) copy-start(f32[2,50]{1,0:T(2,128)} %param.36) | copy-start | bytes 1204
  118.9 26.8 %all-to-all-start.3 = ((bf16[16,2,4608]{2,1,0:T(2,128)(2,1)}), bf16[16,2,4608]{2,1,0:T(2,128)(2,1)S(1)}, u32[]{:S(2)}, u32[]{:S(2)}) async-start(bf16[16,2,4608]{2,1,0:T(2,128)(2,1)} %reshape.362), calls=%async_computation.3 | async-start | bytes 589824 | tf_op jit(solution)/shard_map/all_to_all | solution.py:73
  148.7 1.0 copy-start.2
  149.2 0.9 copy-start.29
  149.7 4.7 %copy-start.14 = (f32[48,64]{1,0:T(8,128)S(1)}, f32[48,64]{1,0:T(8,128)}, u32[]{:S(2)}) copy-start(f32[48,64]{1,0:T(8,128)} %param.35) | copy-start | bytes 36868
  149.7 4.7 %copy-start.17 = (pred[48]{0:T(512)(128)(4,1)S(1)}, pred[48]{0:T(512)(128)(4,1)}, u32[]{:S(2)}) copy-start(pred[48]{0:T(512)(128)(4,1)} %copy-done.15) | copy-start | bytes 148
  150.6 3.8 %collective-permute-start.1 = (f32[48,32]{1,0:T(8,128)S(1)}, f32[48,32]{1,0:T(8,128)S(1)}, u32[]{:S(2)}, u32[]{:S(2)}) collective-permute-start(f32[48,32]{1,0:T(8,128)S(1)} %constant_dynamic-slice_fusion), channel_id=1, source_target_pairs={{0,16},{16,0},{1,17},{17,1},{2,18},{18,2},{3,19},{19,3},{4,20},{20... | collective-permute-start | bytes 18440 | tf_op jit(solution)/shard_map/ppermute | solution.py:16
  (5 other events, 3.6 us)
Sparse Core Ops, SparseCore 0:
  68.3 43.3 all-gather.2

commit v2 on v1

--- a/solution.py
+++ b/solution.py
@@ -1,9 +1,12 @@
+import functools
 import math
 
 import jax
 import jax.numpy as jnp
 import numpy as np
 from jax import lax
+from jax.experimental import pallas as pl
+from jax.experimental.pallas import tpu as pltpu
 from jax.sharding import PartitionSpec as P
 
 TEXT_SLOTS = 256
@@ -87,6 +90,305 @@
         attended_rows,
         lax.all_gather(out_weight, ("cfg", "seq"), axis=1, tiled=True),
         preferred_element_type=jnp.float32,
+    )
+
+
+LANES = 128
+
+
+def each(count, body, first=0):
+    def step(index, carry):
+        body(index)
+        return carry
+
+    lax.fori_loop(first, count, step, 0)
+
+
+def dot32(left, right):
+    return jnp.dot(left, right, preferred_element_type=jnp.float32)
+
+
+def norm_turn(ref, gain, offset, cosine, sine_part, group_count, factor):
+    rows = ref.shape[0]
+    values = jnp.concatenate(
+        [ref[:, g * LANES : (g + 1) * LANES] for g in range(group_count)], axis=0
+    )
+    down = lax.broadcasted_iota(jnp.int32, (LANES, LANES), 0) < 64
+    across = lax.broadcasted_iota(jnp.int32, (LANES, LANES), 1) < 64
+    average = jnp.where(down == across, 1.0 / 64, 0.0).astype(jnp.bfloat16)
+    centred = values.astype(jnp.float32) - dot32(values, average)
+    square = centred * centred
+    high = square.astype(jnp.bfloat16)
+    low = (square - high.astype(jnp.float32)).astype(jnp.bfloat16)
+    variance = dot32(high, average) + dot32(low, average)
+    normed = centred * lax.rsqrt(variance + 1e-06) * gain + offset
+    even = lax.broadcasted_iota(jnp.int32, normed.shape, 1) % 2 == 0
+    beside = jnp.where(even, -pltpu.roll(normed, LANES - 1, 1), pltpu.roll(normed, 1, 1))
+    normed = normed.reshape(group_count, rows, LANES)
+    beside = beside.reshape(group_count, rows, LANES)
+    turned = normed * cosine[None] + beside * sine_part[None]
+    return (turned * factor).astype(jnp.bfloat16)
+
+
+def step_kernel(
+    seq_count,
+    text_len, step_index, solver_coef,
+    hidden, queries, key_proj, value_proj, heads_norm, angles, time_embed, gate_table, mod_table,
+    out_weight, proj_weight, proj_bias, latent,
+    out,
+    v_send, v_recv, qk_send, qk_recv, vec, partner_weight, every, part, back, total, gate_full,
+    pred_send, pred_recv,
+    v_sem, qk_sem, vec_sem, z_sem, x_sem, core_sem, back_sem, pair_sem,
+):
+    me = lax.axis_index("seq")
+    cfg = lax.axis_index("cfg")
+    layers = seq_count // 4
+    layer, in_layer = me // 4, me % 4
+    x_peer = me + 2 - 4 * ((me // 2) % 2)
+    core_peer = me + 1 - 2 * (me % 2)
+    rows = queries.shape[0]
+    all_rows = seq_count * rows
+    own_width = out_weight.shape[1]
+    model_width = hidden.shape[1]
+
+    barrier = pltpu.get_barrier_semaphore()
+
+    def greet(d):
+        pl.semaphore_signal(
+            barrier, inc=1, device_id=(cfg, (me + d) % seq_count),
+            device_id_type=pl.DeviceIdType.MESH,
+        )
+
+    each(seq_count, greet, 1)
+    pl.semaphore_signal(
+        barrier, inc=1, device_id=(1 - cfg, me), device_id_type=pl.DeviceIdType.MESH
+    )
+    for g in range(seq_count):
+        v_send[g] = value_proj[:, g * LANES : (g + 1) * LANES]
+    pl.semaphore_wait(barrier, seq_count)
+
+    def remote(src, dst, sems, index, where):
+        return pltpu.make_async_remote_copy(
+            src_ref=src, dst_ref=dst, send_sem=sems.at[0, index], recv_sem=sems.at[1, index],
+            device_id=where, device_id_type=pl.DeviceIdType.MESH,
+        )
+
+    def peer(d):
+        return (me + d) % seq_count
+
+    def v_copy(d):
+        return remote(v_send.at[peer(d)], v_recv.at[me], v_sem, d, (cfg, peer(d)))
+
+    def qk_copy(d):
+        return remote(qk_send.at[peer(d)], qk_recv.at[me], qk_sem, d, (cfg, peer(d)))
+
+    def vec_copy(d):
+        return remote(vec.at[me], vec.at[me], vec_sem, d, (cfg, peer(d)))
+
+    def back_copy(d):
+        return remote(part.at[peer(d)], back.at[me], back_sem, d, (cfg, peer(d)))
+
+    each(seq_count, lambda d: v_copy(d).start(), 1)
+    weight_copy = remote(out_weight, partner_weight, pair_sem, 0, (1 - cfg, me))
+    weight_copy.start()
+
+    cosine = jnp.cos(angles[...])
+    sine_part = jnp.sin(angles[...])
+    qk_send[:, 1] = norm_turn(
+        key_proj, heads_norm[1:2], heads_norm[3:4], cosine, sine_part, seq_count, 1.0
+    )
+    qk_send[:, 0] = norm_turn(
+        queries, heads_norm[0:1], heads_norm[2:3], cosine, sine_part, seq_count, 0.125
+    )
+    each(seq_count, lambda d: qk_copy(d).start(), 1)
+    v_recv[me] = v_send[me]
+    qk_recv[me] = qk_send[me]
+
+    embed = time_embed[...].astype(jnp.float32)
+    embed = (embed * (1.0 / (1.0 + jnp.exp(-embed)))).astype(jnp.bfloat16)
+    embed = jnp.broadcast_to(embed, (16, embed.shape[1]))
+    gate_width = gate_table.shape[1]
+    vec[me, :, 0:gate_width] = dot32(embed, gate_table[...])[0:1]
+    vec[me, :, 256:] = dot32(embed, mod_table[...])[0:1]
+    each(seq_count, lambda d: vec_copy(d).start(), 1)
+
+    each(seq_count, lambda d: v_copy(d).wait(), 1)
+    each(seq_count, lambda d: qk_copy(d).wait(), 1)
+
+    keys = qk_recv[:, 1].reshape(all_rows, LANES)
+    values = v_recv[...].reshape(all_rows, LANES)
+    key_index = lax.broadcasted_iota(jnp.int32, (1, all_rows), 1)
+    valid = (key_index >= TEXT_SLOTS) | (key_index < text_len[0])
+    piece = 4
+
+    def attend(index):
+        asked = qk_recv[pl.ds(index * piece, piece), 0].reshape(piece * rows, LANES)
+        lane = lax.broadcasted_iota(jnp.int32, asked.shape, 1)
+        results = []
+        for head in range(2):
+            own = jnp.where((lane >= 64) == (head == 1), asked, jnp.zeros_like(asked))
+            scores = lax.dot_general(
+                own, keys, (((1,), (1,)), ((), ())), preferred_element_type=jnp.float32
+            )
+            weights = jnp.where(valid, jnp.exp(scores), 0.0)
+            denominator = jnp.sum(weights, axis=1, keepdims=True)
+            results.append(dot32(weights.astype(jnp.bfloat16), values) / denominator)
+        both = jnp.where(lane < 64, results[0], results[1]).astype(jnp.bfloat16)
+        start = pl.multiple_of(index * piece * rows, piece * rows)
+        every[me, pl.ds(start, piece * rows), :] = both
+
+    each(seq_count // piece, attend)
+
+    def line(d):
+        return (layer + layers - d) % layers * 4
+
+    def z_copy(d):
+        target = (layer + d) % layers * 4 + in_layer
+        return remote(every.at[me], every.at[me], z_sem, d, (cfg, target))
+
+    def x_copy(d):
+        block = every.at[line(d) + in_layer]
+        return remote(block, block, x_sem, d, (cfg, x_peer))
+
+    def core_copy(d):
+        block = every.at[line(d) + in_layer]
+        return remote(block, block, core_sem, d, (cfg, core_peer))
+
+    def cross_copy(d):
+        block = every.at[line(d) + x_peer % 4]
+        return remote(block, block, core_sem, layers + d, (cfg, core_peer))
+
+    each(layers, lambda d: z_copy(layers - d).start(), 1)
+    x_copy(0).start()
+    core_copy(0).start()
+    for d in range(layers):
+        if d > 0:
+            z_copy(d).wait_recv()
+            x_copy(d).start()
+            core_copy(d).start()
+        if d > 0:
+            x_copy(d - 1).wait_recv()
+            cross_copy(d - 1).start()
+    x_copy(layers - 1).wait_recv()
+    cross_copy(layers - 1).start()
+    weight_copy.wait()
+    each(layers, lambda d: core_copy(d).wait_recv())
+    each(layers, lambda d: cross_copy(d).wait_recv())
+
+    def project(index):
+        start = pl.multiple_of(index * piece * rows, piece * rows)
+        asked = jnp.concatenate(
+            [every[g, pl.ds(start, piece * rows), :] for g in range(seq_count)], axis=1
+        )
+        shape = (piece, rows, own_width)
+        place = pl.ds(index * piece, piece)
+        part[place, cfg] = dot32(asked, out_weight[...]).astype(jnp.bfloat16).reshape(shape)
+        part[place, 1 - cfg] = (
+            dot32(asked, partner_weight[...]).astype(jnp.bfloat16).reshape(shape)
+        )
+
+    each(seq_count // piece, project)
+    each(seq_count, lambda d: back_copy(d).start(), 1)
+    back[me] = part[me]
+    each(seq_count, lambda d: vec_copy(d).wait(), 1)
+    for g in range(seq_count):
+        gate_full[:, g * gate_width : (g + 1) * gate_width] = vec[g, :, 0:gate_width]
+    each(layers, lambda d: z_copy(d).wait_send(), 1)
+    each(layers, lambda d: x_copy(d).wait_send())
+    each(layers, lambda d: core_copy(d).wait_send())
+    each(layers, lambda d: cross_copy(d).wait_send())
+    each(seq_count, lambda d: back_copy(d).wait(), 1)
+
+    for half in range(2):
+        for g in range(seq_count):
+            first = (half * seq_count + g) * own_width
+            total[:, first : first + own_width] = back[g, half].astype(jnp.float32)
+    residual = hidden[...].astype(jnp.float32) + gate_full[...] * total[...]
+    centred = residual - jnp.mean(residual, axis=1, keepdims=True)
+    variance = jnp.mean(centred * centred, axis=1, keepdims=True)
+    normed = centred * lax.rsqrt(variance + 1e-05)
+    half_count = seq_count // 2
+    shift = jnp.concatenate([vec[g, :, 256:] for g in range(half_count)], axis=1)
+    scale = jnp.concatenate([vec[half_count + g, :, 256:] for g in range(half_count)], axis=1)
+    normed = (normed * (1.0 + scale) + shift).astype(jnp.bfloat16)
+    prediction = dot32(normed, proj_weight[...]) + proj_bias[...]
+    width = prediction.shape[1] // 2
+    is_cond = cfg == 0
+    left, right = prediction[:, :width], prediction[:, width:]
+    own = jnp.where(is_cond, left, right)
+    pred_send[...] = jnp.where(is_cond, right, left)
+    pred_copy = remote(pred_send, pred_recv, pair_sem, 1, (1 - cfg, me))
+    pred_copy.start()
+    pred_copy.wait()
+    other = pred_recv[...]
+    cond = jnp.where(is_cond, own, other)
+    uncond = jnp.where(is_cond, other, own)
+    guided = uncond + GUIDANCE * (cond - uncond)
+    own_latent = jnp.where(is_cond, latent[:, :width], latent[:, width:])
+    at = step_index[0]
+    updated = solver_coef[0, at] * own_latent + solver_coef[1, at] * guided
+    row = me * rows + lax.broadcasted_iota(jnp.int32, updated.shape, 0)
+    out[...] = jnp.where(row >= TEXT_SLOTS, updated, 0.0)
+
+
+def in_one_kernel(
+    hidden, queries, key_proj, value_proj, norm_gain, norm_bias, positions, text_len, time_embed,
+    gate_table, mod_table, out_weight, proj_weight, proj_bias, latent, solver_coef, step_index,
+):
+    seq_count = lax.axis_size("seq")
+    rows = queries.shape[1]
+    row_index = lax.axis_index("seq") * rows + jnp.arange(rows)
+    angles = jnp.where((row_index >= TEXT_SLOTS)[:, None], rotary_angles(positions), 0.0)
+    angles = jnp.tile(jnp.repeat(angles, 2, axis=1), (1, 2))
+    heads_norm = jnp.tile(jnp.concatenate([norm_gain, norm_bias], axis=0), (1, 2))
+    own_width = out_weight.shape[1]
+    model_width = hidden.shape[2]
+    bf16, f32 = jnp.bfloat16, jnp.float32
+    vec_width = 256 + mod_table.shape[1]
+    out_width = latent.shape[1] // 2
+    in_vmem = pl.BlockSpec(memory_space=pltpu.VMEM)
+    in_smem = pl.BlockSpec(memory_space=pltpu.SMEM)
+
+    def sems(count):
+        return pltpu.SemaphoreType.DMA((2, count))
+
+    return pl.pallas_call(
+        functools.partial(step_kernel, seq_count),
+        out_shape=jax.ShapeDtypeStruct((rows, out_width), f32),
+        in_specs=[in_smem] * 3 + [in_vmem] * 13,
+        out_specs=in_vmem,
+        scratch_shapes=[
+            pltpu.VMEM((seq_count, rows, LANES), bf16),
+            pltpu.VMEM((seq_count, rows, LANES), bf16),
+            pltpu.VMEM((seq_count, 2, rows, LANES), bf16),
+            pltpu.VMEM((seq_count, 2, rows, LANES), bf16),
+            pltpu.VMEM((seq_count, 1, vec_width), f32),
+            pltpu.VMEM(out_weight.shape, bf16),
+            pltpu.VMEM((seq_count, seq_count * rows, LANES), bf16),
+            pltpu.VMEM((seq_count, 2, rows, own_width), bf16),
+            pltpu.VMEM((seq_count, 2, rows, own_width), bf16),
+            pltpu.VMEM((rows, model_width), f32),
+            pltpu.VMEM((1, model_width), f32),
+            pltpu.VMEM((rows, out_width), f32),
+            pltpu.VMEM((rows, out_width), f32),
+            sems(seq_count),
+            sems(seq_count),
+            sems(seq_count),
+            sems(seq_count // 4),
+            sems(seq_count // 4),
+            sems(seq_count // 2),
+            sems(seq_count),
+            sems(2),
+        ],
+        compiler_params=pltpu.CompilerParams(
+            collective_id=0, has_side_effects=True, vmem_limit_bytes=40 * 1024 * 1024
+        ),
+        name="sampling_step",
+    )(
+        text_len, step_index, solver_coef,
+        hidden[0], queries[0], key_proj[0], value_proj[0], heads_norm, angles,
+        time_embed[None, :], gate_table, mod_table, out_weight, proj_weight, proj_bias[None, :],
+        latent,
     )
 
 
@@ -117,6 +419,12 @@
     row_split = max(seq_count // head_count, 1)
     part_rows = local_rows // row_split
     head_sets = head_count // head_group
+    if head_group * 64 == LANES and seq_count % 4 == 0 and local_rows % 16 == 0:
+        return in_one_kernel(
+            hidden, queries, key_proj, value_proj, norm_gain, norm_bias, positions, text_len,
+            time_embed, gate_table, mod_table, out_weight, proj_weight, proj_bias, latent,
+            solver_coef, step_index,
+        )
     row_index = seq_place * local_rows + jnp.arange(local_rows)
     is_video = row_index >= TEXT_SLOTS
     angles = rotary_angles(positions)

time: 164 us -> 78.5 us (0.48)
  the two profiles are of different devices: /device:TPU:0 before, /device:TPU:3 now
where the time goes in v2:
time: 78.5 us; the launch traced here: 77.3 us
  Pallas kernels  69.6 us (89%)
  local copies, waits for them, and re-layouts  4 us (5%)
  other arithmetic  2.2 us (3%)
  between operations  1.46 us (2%)
    pallas_call x1, Pallas kernels, in_one_kernel(): pl.pallas_call(functools.partial(step_kernel, seq_count), out_shape=jax.S...  69.6 us
    unnamed x27, local copies, waits for them, and re-layouts  2.28 us

profile of v2, /device:TPU:3, one launch (start us, length us, event | category | flops | bytes accessed | tf_op | source)
XLA Modules:
  0.0 77.3 jit_solution(12302939492864833592)
XLA Ops:
  0.0 0.0 copy-start.11
  0.0 0.0 copy-start.10
  1.4 0.7 pad_maximum_fusion
  2.1 0.1 tile.20.heads_norm
  2.2 0.7 convert_element_type.3
  2.8 0.7 broadcast_in_dim.28.time_embed
  3.6 0.0 copy-done.11
  3.6 0.1 broadcast_multiply_fusion.2
  3.7 0.7 broadcast_multiply_fusion.1
  4.4 0.1 copy.24
  4.5 0.1 tile.23.angles
  4.6 0.0 copy-done.10
  4.6 0.1 copy.25.gate_table
  4.8 0.0 copy-done.8
  4.8 0.0 copy-start.9
  4.8 0.0 copy-start.4
  4.8 0.3 copy.26.out_weight
  5.1 0.7 copy-done.9
  5.8 0.0 copy-start.5
  5.8 0.0 copy-start.6
  5.8 0.0 copy-start.7
  5.8 0.4 copy.27.proj_weight
  6.2 0.0 copy-done.4
  6.2 0.6 copy-done
  6.8 0.1 copy-done.1
  6.9 0.1 copy-done.2
  6.9 0.1 copy-done.3
  7.0 0.0 copy-done.5
  7.0 0.0 copy-done.6
  7.0 0.0 copy-done.7
  7.0 69.6 %sampling_step.1 = f32[48,32]{1,0:T(8,128)S(1)} custom-call(s32[1]{0:T(128)S(6)} %copy.29.text_len, s32[1]{0:T(128)S(6)} %copy.30.step_index, f32[2,50]{1,0:T(2,128)S(1)} %copy-done.6, bf16[48,3072]{1,0:T(8,128)(2,1)S(1)} %bitcast.12, bf16[48,2048]{1,0:T(8,128)(2,1)S(1)} %bitcast.13, bf16[48,2048]{1,0:T(8,128)(2,1)S(1)} %bitcast.14, ...), custom_call_target="tpu_custom_call" | custom-call | tf_op jit(solution)/shard_map/sampling_step/pallas_call | solution.py:355
  76.6 0.7 copy.28
  (11 shorter events, 0.1 us)
Async XLA Ops:
  0.0 3.6 %copy-start.11 = (f32[8]{0:T(128)S(1)}, f32[8]{0:T(128)}, u32[]{:S(2)}) copy-start(f32[8]{0:T(128)} %constant.14.clone) | copy-start | bytes 100
  0.0 4.6 %copy-start.10 = (bf16[512,192]{0,1:T(8,128)(2,1)S(1)}, bf16[512,192]{0,1:T(8,128)(2,1)}, u32[]{:S(2)}) copy-start(bf16[512,192]{0,1:T(8,128)(2,1)} %param.28) | copy-start | bytes 589828
  2.8 1.9 %copy-start.8 = (bf16[2048,96]{0,1:T(8,128)(2,1)S(1)}, bf16[2048,96]{0,1:T(8,128)(2,1)}, u32[]{:S(2)}) copy-start(bf16[2048,96]{0,1:T(8,128)(2,1)} %param.30) | copy-start | bytes 1179652
  4.8 1.0 %copy-start.9 = (bf16[3072,64]{0,1:T(8,128)(2,1)S(1)}, bf16[3072,64]{0,1:T(8,128)(2,1)}, u32[]{:S(2)}) copy-start(bf16[3072,64]{0,1:T(8,128)(2,1)} %param.31) | copy-start | bytes 1179652
  4.8 1.4 %copy-start.4 = (bf16[1,48,2048]{2,1,0:T(8,128)(2,1)S(1)}, bf16[1,48,2048]{2,1,0:T(8,128)(2,1)}, u32[]{:S(2)}) copy-start(bf16[1,48,2048]{2,1,0:T(8,128)(2,1)} %param.22) | copy-start | bytes 589828
  5.8 1.0 %copy-start = (bf16[512,384]{1,0:T(8,128)(2,1)S(1)}, bf16[512,384]{1,0:T(8,128)(2,1)}, u32[]{:S(2)}) copy-start(bf16[512,384]{1,0:T(8,128)(2,1)} %mod_table.1) | copy-start | bytes 1179652
  5.8 1.1 %copy-start.1 = (bf16[1,48,3072]{2,1,0:T(8,128)(2,1)S(1)}, bf16[1,48,3072]{2,1,0:T(8,128)(2,1)}, u32[]{:S(2)}) copy-start(bf16[1,48,3072]{2,1,0:T(8,128)(2,1)} %param.19) | copy-start | bytes 884740
  5.8 1.1 %copy-start.2 = (bf16[1,48,2048]{2,1,0:T(8,128)(2,1)S(1)}, bf16[1,48,2048]{2,1,0:T(8,128)(2,1)}, u32[]{:S(2)}) copy-start(bf16[1,48,2048]{2,1,0:T(8,128)(2,1)} %param.20) | copy-start | bytes 589828
  5.8 1.2 %copy-start.3 = (bf16[1,48,2048]{2,1,0:T(8,128)(2,1)S(1)}, bf16[1,48,2048]{2,1,0:T(8,128)(2,1)}, u32[]{:S(2)}) copy-start(bf16[1,48,2048]{2,1,0:T(8,128)(2,1)} %param.21) | copy-start | bytes 589828
  5.8 1.2 %copy-start.5 = (f32[48,64]{1,0:T(8,128)S(1)}, f32[48,64]{1,0:T(8,128)}, u32[]{:S(2)}) copy-start(f32[48,64]{1,0:T(8,128)} %latent.1) | copy-start | bytes 36868
  5.8 1.2 %copy-start.6 = (f32[2,50]{1,0:T(2,128)S(1)}, f32[2,50]{1,0:T(2,128)}, u32[]{:S(2)}) copy-start(f32[2,50]{1,0:T(2,128)} %solver_coef.1) | copy-start | bytes 1204
  5.8 1.2 %copy-start.7 = (f32[64]{0:T(128)S(1)}, f32[64]{0:T(128)}, u32[]{:S(2)}) copy-start(f32[64]{0:T(128)} %param.32) | copy-start | bytes 772

commit v3 on v2

--- a/solution.py
+++ b/solution.py
@@ -108,6 +108,12 @@
     return jnp.dot(left, right, preferred_element_type=jnp.float32)
 
 
+def dot_rows(left, right):
+    return lax.dot_general(
+        left, right, (((1,), (1,)), ((), ())), preferred_element_type=jnp.float32
+    )
+
+
 def norm_turn(ref, gain, offset, cosine, sine_part, group_count, factor):
     rows = ref.shape[0]
     values = jnp.concatenate(
@@ -133,12 +139,12 @@
 def step_kernel(
     seq_count,
     text_len, step_index, solver_coef,
-    hidden, queries, key_proj, value_proj, heads_norm, angles, time_embed, gate_table, mod_table,
-    out_weight, proj_weight, proj_bias, latent,
+    hidden, queries, key_proj, value_proj, norm_gain, norm_bias, positions, frequency, time_embed,
+    gate_table, mod_table, out_weight, proj_weight, proj_bias, latent,
     out,
-    v_send, v_recv, qk_send, qk_recv, vec, partner_weight, every, part, back, total, gate_full,
+    v_send, v_recv, k_send, k_recv, q_send, q_recv, vec, partner_weight, every, part, back, total, gate_full,
     pred_send, pred_recv,
-    v_sem, qk_sem, vec_sem, z_sem, x_sem, core_sem, back_sem, pair_sem,
+    v_sem, k_sem, q_sem, vec_sem, z_sem, x_sem, core_sem, back_sem, pair_sem,
 ):
     me = lax.axis_index("seq")
     cfg = lax.axis_index("cfg")
@@ -148,8 +154,7 @@
     core_peer = me + 1 - 2 * (me % 2)
     rows = queries.shape[0]
     all_rows = seq_count * rows
-    own_width = out_weight.shape[1]
-    model_width = hidden.shape[1]
+    own_width = out_weight.shape[0]
 
     barrier = pltpu.get_barrier_semaphore()
 
@@ -165,6 +170,20 @@
     )
     for g in range(seq_count):
         v_send[g] = value_proj[:, g * LANES : (g + 1) * LANES]
+    lane = lax.broadcasted_iota(jnp.int32, (rows, LANES), 1)
+    row = me * rows + lax.broadcasted_iota(jnp.int32, (rows, LANES), 0)
+    pair = lane % 64
+    place = jnp.where(
+        pair < 16, positions[:, 0:1], jnp.where(pair < 40, positions[:, 1:2], positions[:, 2:3])
+    )
+    angles = jnp.where(row >= TEXT_SLOTS, place.astype(jnp.float32) * frequency[...], 0.0)
+    cosine = jnp.cos(angles)
+    sine_part = jnp.sin(angles)
+    gain = jnp.concatenate([norm_gain[...], norm_gain[...]], axis=1)
+    offset = jnp.concatenate([norm_bias[...], norm_bias[...]], axis=1)
+    k_send[...] = norm_turn(
+        key_proj, gain[1:2], offset[1:2], cosine, sine_part, seq_count, 1.0
+    )
     pl.semaphore_wait(barrier, seq_count)
 
     def remote(src, dst, sems, index, where):
@@ -179,8 +198,11 @@
     def v_copy(d):
         return remote(v_send.at[peer(d)], v_recv.at[me], v_sem, d, (cfg, peer(d)))
 
-    def qk_copy(d):
-        return remote(qk_send.at[peer(d)], qk_recv.at[me], qk_sem, d, (cfg, peer(d)))
+    def k_copy(d):
+        return remote(k_send.at[peer(d)], k_recv.at[me], k_sem, d, (cfg, peer(d)))
+
+    def q_copy(d):
+        return remote(q_send.at[peer(d)], q_recv.at[me], q_sem, d, (cfg, peer(d)))
 
     def vec_copy(d):
         return remote(vec.at[me], vec.at[me], vec_sem, d, (cfg, peer(d)))
@@ -189,114 +211,128 @@
         return remote(part.at[peer(d)], back.at[me], back_sem, d, (cfg, peer(d)))
 
     each(seq_count, lambda d: v_copy(d).start(), 1)
+    each(seq_count, lambda d: k_copy(d).start(), 1)
+    q_send[...] = norm_turn(
+        queries, gain[0:1], offset[0:1], cosine, sine_part, seq_count, 0.125
+    )
+    each(seq_count, lambda d: q_copy(d).start(), 1)
     weight_copy = remote(out_weight, partner_weight, pair_sem, 0, (1 - cfg, me))
     weight_copy.start()
-
-    cosine = jnp.cos(angles[...])
-    sine_part = jnp.sin(angles[...])
-    qk_send[:, 1] = norm_turn(
-        key_proj, heads_norm[1:2], heads_norm[3:4], cosine, sine_part, seq_count, 1.0
-    )
-    qk_send[:, 0] = norm_turn(
-        queries, heads_norm[0:1], heads_norm[2:3], cosine, sine_part, seq_count, 0.125
-    )
-    each(seq_count, lambda d: qk_copy(d).start(), 1)
     v_recv[me] = v_send[me]
-    qk_recv[me] = qk_send[me]
+    k_recv[me] = k_send[me]
+    q_recv[me] = q_send[me]
 
     embed = time_embed[...].astype(jnp.float32)
     embed = (embed * (1.0 / (1.0 + jnp.exp(-embed)))).astype(jnp.bfloat16)
     embed = jnp.broadcast_to(embed, (16, embed.shape[1]))
-    gate_width = gate_table.shape[1]
-    vec[me, :, 0:gate_width] = dot32(embed, gate_table[...])[0:1]
+    gate_width = gate_table.shape[0]
+    vec[me, :, 0:gate_width] = dot_rows(embed, gate_table[...])[0:1]
     vec[me, :, 256:] = dot32(embed, mod_table[...])[0:1]
     each(seq_count, lambda d: vec_copy(d).start(), 1)
 
     each(seq_count, lambda d: v_copy(d).wait(), 1)
-    each(seq_count, lambda d: qk_copy(d).wait(), 1)
-
-    keys = qk_recv[:, 1].reshape(all_rows, LANES)
+    each(seq_count, lambda d: k_copy(d).wait(), 1)
+    each(seq_count, lambda d: q_copy(d).wait(), 1)
+
+    keys = k_recv[...].reshape(all_rows, LANES)
     values = v_recv[...].reshape(all_rows, LANES)
     key_index = lax.broadcasted_iota(jnp.int32, (1, all_rows), 1)
     valid = (key_index >= TEXT_SLOTS) | (key_index < text_len[0])
-    piece = 4
-
-    def attend(index):
-        asked = qk_recv[pl.ds(index * piece, piece), 0].reshape(piece * rows, LANES)
+
+    def attend(piece):
+        asked = jnp.concatenate([q_recv[4 * at + piece] for at in range(layers)], axis=0)
         lane = lax.broadcasted_iota(jnp.int32, asked.shape, 1)
         results = []
         for head in range(2):
             own = jnp.where((lane >= 64) == (head == 1), asked, jnp.zeros_like(asked))
-            scores = lax.dot_general(
-                own, keys, (((1,), (1,)), ((), ())), preferred_element_type=jnp.float32
-            )
-            weights = jnp.where(valid, jnp.exp(scores), 0.0)
+            weights = jnp.where(valid, jnp.exp(dot_rows(own, keys)), 0.0)
             denominator = jnp.sum(weights, axis=1, keepdims=True)
             results.append(dot32(weights.astype(jnp.bfloat16), values) / denominator)
-        both = jnp.where(lane < 64, results[0], results[1]).astype(jnp.bfloat16)
-        start = pl.multiple_of(index * piece * rows, piece * rows)
-        every[me, pl.ds(start, piece * rows), :] = both
-
-    each(seq_count // piece, attend)
+        every[me, piece] = jnp.where(lane < 64, results[0], results[1]).astype(jnp.bfloat16)
 
     def line(d):
         return (layer + layers - d) % layers * 4
 
-    def z_copy(d):
+    def z_copy(piece, d):
         target = (layer + d) % layers * 4 + in_layer
-        return remote(every.at[me], every.at[me], z_sem, d, (cfg, target))
-
-    def x_copy(d):
-        block = every.at[line(d) + in_layer]
-        return remote(block, block, x_sem, d, (cfg, x_peer))
-
-    def core_copy(d):
-        block = every.at[line(d) + in_layer]
-        return remote(block, block, core_sem, d, (cfg, core_peer))
-
-    def cross_copy(d):
-        block = every.at[line(d) + x_peer % 4]
-        return remote(block, block, core_sem, layers + d, (cfg, core_peer))
-
-    each(layers, lambda d: z_copy(layers - d).start(), 1)
-    x_copy(0).start()
-    core_copy(0).start()
-    for d in range(layers):
-        if d > 0:
-            z_copy(d).wait_recv()
-            x_copy(d).start()
-            core_copy(d).start()
-        if d > 0:
-            x_copy(d - 1).wait_recv()
-            cross_copy(d - 1).start()
-    x_copy(layers - 1).wait_recv()
-    cross_copy(layers - 1).start()
+        block = every.at[me, piece]
+        return remote(block, block, z_sem, piece * layers + d, (cfg, target))
+
+    def x_copy(piece, d):
+        block = every.at[line(d) + in_layer, piece]
+        return remote(block, block, x_sem, piece * layers + d, (cfg, x_peer))
+
+    def core_copy(piece, d):
+        block = every.at[line(d) + in_layer, piece]
+        return remote(block, block, core_sem, piece * layers + d, (cfg, core_peer))
+
+    def cross_copy(piece, d):
+        block = every.at[line(d) + x_peer % 4, piece]
+        return remote(block, block, core_sem, (4 + piece) * layers + d, (cfg, core_peer))
+
+    def give(piece):
+        each(layers, lambda d: z_copy(piece, layers - d).start(), 1)
+        x_copy(piece, 0).start()
+        core_copy(piece, 0).start()
+
+    def forward(piece):
+        def from_line(d):
+            z_copy(piece, d).wait_recv()
+            x_copy(piece, d).start()
+            core_copy(piece, d).start()
+            x_copy(piece, d - 1).wait_recv()
+            cross_copy(piece, d - 1).start()
+
+        each(layers, from_line, 1)
+        x_copy(piece, layers - 1).wait_recv()
+        cross_copy(piece, layers - 1).start()
+
+    def project(piece):
+        each(layers, lambda d: core_copy(piece, d).wait_recv())
+        each(layers, lambda d: cross_copy(piece, d).wait_recv())
+        asked = jnp.concatenate([every[g, piece] for g in range(seq_count)], axis=1)
+        shape = (layers, rows, own_width)
+        own = dot_rows(asked, out_weight[...]).astype(jnp.bfloat16).reshape(shape)
+        other = dot_rows(asked, partner_weight[...]).astype(jnp.bfloat16).reshape(shape)
+        for at in range(layers):
+            part[4 * at + piece, cfg] = own[at]
+            part[4 * at + piece, 1 - cfg] = other[at]
+
+        def hand_back(at):
+            d = (4 * at + piece + seq_count - me) % seq_count
+
+            @pl.when(d != 0)
+            def _():
+                back_copy(d).start()
+
+        each(layers, hand_back)
+
+    attend(0)
+    give(0)
+    attend(1)
+    give(1)
+    attend(2)
+    give(2)
+    forward(0)
+    attend(3)
+    give(3)
+    forward(1)
     weight_copy.wait()
-    each(layers, lambda d: core_copy(d).wait_recv())
-    each(layers, lambda d: cross_copy(d).wait_recv())
-
-    def project(index):
-        start = pl.multiple_of(index * piece * rows, piece * rows)
-        asked = jnp.concatenate(
-            [every[g, pl.ds(start, piece * rows), :] for g in range(seq_count)], axis=1
-        )
-        shape = (piece, rows, own_width)
-        place = pl.ds(index * piece, piece)
-        part[place, cfg] = dot32(asked, out_weight[...]).astype(jnp.bfloat16).reshape(shape)
-        part[place, 1 - cfg] = (
-            dot32(asked, partner_weight[...]).astype(jnp.bfloat16).reshape(shape)
-        )
-
-    each(seq_count // piece, project)
-    each(seq_count, lambda d: back_copy(d).start(), 1)
+    forward(2)
+    project(0)
+    forward(3)
+    project(1)
+    project(2)
+    project(3)
     back[me] = part[me]
     each(seq_count, lambda d: vec_copy(d).wait(), 1)
     for g in range(seq_count):
         gate_full[:, g * gate_width : (g + 1) * gate_width] = vec[g, :, 0:gate_width]
-    each(layers, lambda d: z_copy(d).wait_send(), 1)
-    each(layers, lambda d: x_copy(d).wait_send())
-    each(layers, lambda d: core_copy(d).wait_send())
-    each(layers, lambda d: cross_copy(d).wait_send())
+    for piece in range(4):
+        each(layers, lambda d: z_copy(piece, d).wait_send(), 1)
+        each(layers, lambda d: x_copy(piece, d).wait_send())
+        each(layers, lambda d: core_copy(piece, d).wait_send())
+        each(layers, lambda d: cross_copy(piece, d).wait_send())
     each(seq_count, lambda d: back_copy(d).wait(), 1)
 
     for half in range(2):
@@ -311,7 +347,7 @@
     shift = jnp.concatenate([vec[g, :, 256:] for g in range(half_count)], axis=1)
     scale = jnp.concatenate([vec[half_count + g, :, 256:] for g in range(half_count)], axis=1)
     normed = (normed * (1.0 + scale) + shift).astype(jnp.bfloat16)
-    prediction = dot32(normed, proj_weight[...]) + proj_bias[...]
+    prediction = dot_rows(normed, proj_weight[...]) + proj_bias[...]
     width = prediction.shape[1] // 2
     is_cond = cfg == 0
     left, right = prediction[:, :width], prediction[:, width:]
@@ -327,8 +363,8 @@
     own_latent = jnp.where(is_cond, latent[:, :width], latent[:, width:])
     at = step_index[0]
     updated = solver_coef[0, at] * own_latent + solver_coef[1, at] * guided
-    row = me * rows + lax.broadcasted_iota(jnp.int32, updated.shape, 0)
-    out[...] = jnp.where(row >= TEXT_SLOTS, updated, 0.0)
+    out_row = me * rows + lax.broadcasted_iota(jnp.int32, updated.shape, 0)
+    out[...] = jnp.where(out_row >= TEXT_SLOTS, updated, 0.0)
 
 
 def in_one_kernel(
@@ -337,10 +373,10 @@
 ):
     seq_count = lax.axis_size("seq")
     rows = queries.shape[1]
-    row_index = lax.axis_index("seq") * rows + jnp.arange(rows)
-    angles = jnp.where((row_index >= TEXT_SLOTS)[:, None], rotary_angles(positions), 0.0)
-    angles = jnp.tile(jnp.repeat(angles, 2, axis=1), (1, 2))
-    heads_norm = jnp.tile(jnp.concatenate([norm_gain, norm_bias], axis=0), (1, 2))
+    time_freq = 10000.0 ** (-2.0 * np.arange(8) / 16.0)
+    space_freq = 10000.0 ** (-2.0 * np.arange(12) / 24.0)
+    frequency = np.repeat(np.concatenate([time_freq, space_freq, space_freq]), 2)
+    frequency = np.tile(frequency, 2).astype(np.float32)[None, :]
     own_width = out_weight.shape[1]
     model_width = hidden.shape[2]
     bf16, f32 = jnp.bfloat16, jnp.float32
@@ -355,16 +391,18 @@
     return pl.pallas_call(
         functools.partial(step_kernel, seq_count),
         out_shape=jax.ShapeDtypeStruct((rows, out_width), f32),
-        in_specs=[in_smem] * 3 + [in_vmem] * 13,
+        in_specs=[in_smem] * 3 + [in_vmem] * 15,
         out_specs=in_vmem,
         scratch_shapes=[
             pltpu.VMEM((seq_count, rows, LANES), bf16),
             pltpu.VMEM((seq_count, rows, LANES), bf16),
-            pltpu.VMEM((seq_count, 2, rows, LANES), bf16),
-            pltpu.VMEM((seq_count, 2, rows, LANES), bf16),
+            pltpu.VMEM((seq_count, rows, LANES), bf16),
+            pltpu.VMEM((seq_count, rows, LANES), bf16),
+            pltpu.VMEM((seq_count, rows, LANES), bf16),
+            pltpu.VMEM((seq_count, rows, LANES), bf16),
             pltpu.VMEM((seq_count, 1, vec_width), f32),
-            pltpu.VMEM(out_weight.shape, bf16),
-            pltpu.VMEM((seq_count, seq_count * rows, LANES), bf16),
+            pltpu.VMEM(out_weight.shape[::-1], bf16),
+            pltpu.VMEM((seq_count, 4, seq_count // 4 * rows, LANES), bf16),
             pltpu.VMEM((seq_count, 2, rows, own_width), bf16),
             pltpu.VMEM((seq_count, 2, rows, own_width), bf16),
             pltpu.VMEM((rows, model_width), f32),
@@ -374,9 +412,10 @@
             sems(seq_count),
             sems(seq_count),
             sems(seq_count),
-            sems(seq_count // 4),
-            sems(seq_count // 4),
-            sems(seq_count // 2),
+            sems(seq_count),
+            sems(seq_count),
+            sems(seq_count),
+            sems(seq_count * 2),
             sems(seq_count),
             sems(2),
         ],
@@ -386,8 +425,9 @@
         name="sampling_step",
     )(
         text_len, step_index, solver_coef,
-        hidden[0], queries[0], key_proj[0], value_proj[0], heads_norm, angles,
-        time_embed[None, :], gate_table, mod_table, out_weight, proj_weight, proj_bias[None, :],
+        hidden[0], queries[0], key_proj[0], value_proj[0], norm_gain, norm_bias, positions.T,
+        frequency, time_embed[None, :], gate_table.T, mod_table, out_weight.T, proj_weight.T,
+        proj_bias[None, :],
         latent,
     )
 

time: 78.5 us -> 81.5 us (1.038)
  local copies, waits for them, and re-layouts: 4 us -> 9.13 us
  other arithmetic: 2.2 us -> 0 us
    unnamed x27 -> x33, local copies, waits for them, and re-layouts: 2.28 us -> 8.44 us
    pallas_call x1, Pallas kernels: 69.6 us -> 70.4 us  [in_one_kernel(): pl.pallas_call(functools.partial(step_kernel, seq_count), out_shape=jax.S...]
where the time goes in v3:
time: 81.5 us; the launch traced here: 81 us
  Pallas kernels  70.4 us (86%)
  local copies, waits for them, and re-layouts  9.13 us (11%)
  between operations  1.41 us (2%)
    pallas_call x1, Pallas kernels, in_one_kernel(): pl.pallas_call(functools.partial(step_kernel, seq_count), out_shape=jax.S...  70.4 us
    unnamed x33, local copies, waits for them, and re-layouts  8.44 us

profile of v3, /device:TPU:3, one launch (start us, length us, event | category | flops | bytes accessed | tf_op | source)
XLA Modules:
  0.0 81.0 jit_solution(3747771169178096975)
XLA Ops:
  0.0 0.0 copy-start.15
  0.0 0.0 copy-start.14
  0.7 0.0 copy-start.8
  1.3 0.0 copy-done.15
  1.4 0.0 copy-done.14
  1.4 0.0 copy-start.10
  1.4 0.0 copy-start.11
  1.4 0.0 copy-start.13
  1.4 0.1 copy.19
  1.5 0.0 copy-start.12
  1.5 0.0 copy-done.8
  1.5 0.5 copy-done.10
  2.1 0.0 copy-done.11
  2.1 0.0 copy-done.13
  2.1 0.1 copy-done.9
  2.2 0.0 copy-done.12
  2.2 0.0 copy-start
  2.2 1.0 %copy-done = bf16[512,384]{1,0:T(8,128)(2,1)S(1)} copy-done((bf16[512,384]{1,0:T(8,128)(2,1)S(1)}, bf16[512,384]{1,0:T(8,128)(2,1)}, u32[]{:S(2)}) %copy-start) | copy-done | bytes 393240
  3.2 0.0 copy-start.1
  3.2 1.0 %copy-done.1 = bf16[2048,96]{0,1:T(8,128)(2,1)S(1)} copy-done((bf16[2048,96]{0,1:T(8,128)(2,1)S(1)}, bf16[2048,96]{0,1:T(8,128)(2,1)}, u32[]{:S(2)}) %copy-start.1) | copy-done | bytes 393240
  4.2 0.0 copy-start.2
  4.2 1.0 %copy-done.2 = bf16[3072,64]{0,1:T(8,128)(2,1)S(1)} copy-done((bf16[3072,64]{0,1:T(8,128)(2,1)S(1)}, bf16[3072,64]{0,1:T(8,128)(2,1)}, u32[]{:S(2)}) %copy-start.2) | copy-done | bytes 393240
  5.2 0.0 copy-start.3
  5.2 1.0 %copy-done.3 = bf16[1,48,3072]{2,1,0:T(8,128)(2,1)S(1)} copy-done((bf16[1,48,3072]{2,1,0:T(8,128)(2,1)S(1)}, bf16[1,48,3072]{2,1,0:T(8,128)(2,1)}, u32[]{:S(2)}) %copy-start.3) | copy-done | bytes 294936
  6.1 0.0 copy-start.4
  6.1 0.9 %copy-done.4 = bf16[1,48,2048]{2,1,0:T(8,128)(2,1)S(1)} copy-done((bf16[1,48,2048]{2,1,0:T(8,128)(2,1)S(1)}, bf16[1,48,2048]{2,1,0:T(8,128)(2,1)}, u32[]{:S(2)}) %copy-start.4) | copy-done | bytes 196632
  7.1 0.0 copy-start.5
  7.1 0.9 %copy-done.5 = bf16[1,48,2048]{2,1,0:T(8,128)(2,1)S(1)} copy-done((bf16[1,48,2048]{2,1,0:T(8,128)(2,1)S(1)}, bf16[1,48,2048]{2,1,0:T(8,128)(2,1)}, u32[]{:S(2)}) %copy-start.5) | copy-done | bytes 196632
  8.0 0.9 %copy-done.6 = bf16[1,48,2048]{2,1,0:T(8,128)(2,1)S(1)} copy-done((bf16[1,48,2048]{2,1,0:T(8,128)(2,1)S(1)}, bf16[1,48,2048]{2,1,0:T(8,128)(2,1)}, u32[]{:S(2)}) %copy-start.6) | copy-done | bytes 196632
  8.9 0.9 %copy-done.7 = bf16[512,192]{0,1:T(8,128)(2,1)S(1)} copy-done((bf16[512,192]{0,1:T(8,128)(2,1)S(1)}, bf16[512,192]{0,1:T(8,128)(2,1)}, u32[]{:S(2)}) %copy-start.7) | copy-done | bytes 196632
  9.9 70.4 %sampling_step.1 = f32[48,32]{1,0:T(8,128)S(1)} custom-call(s32[1]{0:T(128)S(6)} %copy.21.text_len, s32[1]{0:T(128)S(6)} %copy.22.step_index, f32[2,50]{1,0:T(2,128)S(1)} %copy-done.9, bf16[48,3072]{1,0:T(8,128)(2,1)S(1)} %bitcast.11, bf16[48,2048]{1,0:T(8,128)(2,1)S(1)} %bitcast.12, bf16[48,2048]{1,0:T(8,128)(2,1)S(1)} %bitcast.13, ...), custom_call_target="tpu_custom_call" | custom-call | tf_op jit(solution)/shard_map/sampling_step/pallas_call | solution.py:391
  80.3 0.7 copy.20
  (4 shorter events, 0.0 us)
Async XLA Ops:
  0.0 1.3 %copy-start.15 = (bf16[512]{0:T(512)(128)(2,1)S(1)}, bf16[512]{0:T(512)(128)(2,1)}, u32[]{:S(2)}) copy-start(bf16[512]{0:T(512)(128)(2,1)} %param.26) | copy-start | bytes 3076
  0.0 1.4 %copy-start.14 = (s32[3,48]{1,0:T(4,128)S(1)}, s32[3,48]{1,0:T(4,128)}, u32[]{:S(2)}) copy-start(s32[3,48]{1,0:T(4,128)} %param.24) | copy-start | bytes 1732
  0.7 0.8 %copy-start.8 = (f32[48,64]{1,0:T(8,128)S(1)}, f32[48,64]{1,0:T(8,128)}, u32[]{:S(2)}) copy-start(f32[48,64]{1,0:T(8,128)} %latent.1) | copy-start | bytes 36868
  1.4 0.7 copy-start.10
  1.4 0.7 copy-start.11
  1.4 0.7 copy-start.13
  1.5 0.7 copy-start.9
  1.5 0.7 copy-start.12
  2.2 1.0 %copy-start = (bf16[512,384]{1,0:T(8,128)(2,1)S(1)}, bf16[512,384]{1,0:T(8,128)(2,1)}, u32[]{:S(2)}) copy-start(bf16[512,384]{1,0:T(8,128)(2,1)} %mod_table.1) | copy-start | bytes 1179652
  3.2 1.0 %copy-start.1 = (bf16[2048,96]{0,1:T(8,128)(2,1)S(1)}, bf16[2048,96]{0,1:T(8,128)(2,1)}, u32[]{:S(2)}) copy-start(bf16[2048,96]{0,1:T(8,128)(2,1)} %param.29) | copy-start | bytes 1179652
  4.2 1.0 %copy-start.2 = (bf16[3072,64]{0,1:T(8,128)(2,1)S(1)}, bf16[3072,64]{0,1:T(8,128)(2,1)}, u32[]{:S(2)}) copy-start(bf16[3072,64]{0,1:T(8,128)(2,1)} %param.30) | copy-start | bytes 1179652
  5.2 1.0 %copy-start.3 = (bf16[1,48,3072]{2,1,0:T(8,128)(2,1)S(1)}, bf16[1,48,3072]{2,1,0:T(8,128)(2,1)}, u32[]{:S(2)}) copy-start(bf16[1,48,3072]{2,1,0:T(8,128)(2,1)} %param.18) | copy-start | bytes 884740
  6.1 0.9 %copy-start.4 = (bf16[1,48,2048]{2,1,0:T(8,128)(2,1)S(1)}, bf16[1,48,2048]{2,1,0:T(8,128)(2,1)}, u32[]{:S(2)}) copy-start(bf16[1,48,2048]{2,1,0:T(8,128)(2,1)} %param.19) | copy-start | bytes 589828
  7.1 0.9 %copy-start.5 = (bf16[1,48,2048]{2,1,0:T(8,128)(2,1)S(1)}, bf16[1,48,2048]{2,1,0:T(8,128)(2,1)}, u32[]{:S(2)}) copy-start(bf16[1,48,2048]{2,1,0:T(8,128)(2,1)} %param.20) | copy-start | bytes 589828
  8.0 0.9 %copy-start.6 = (bf16[1,48,2048]{2,1,0:T(8,128)(2,1)S(1)}, bf16[1,48,2048]{2,1,0:T(8,128)(2,1)}, u32[]{:S(2)}) copy-start(bf16[1,48,2048]{2,1,0:T(8,128)(2,1)} %param.21) | copy-start | bytes 589828
  8.9 0.9 %copy-start.7 = (bf16[512,192]{0,1:T(8,128)(2,1)S(1)}, bf16[512,192]{0,1:T(8,128)(2,1)}, u32[]{:S(2)}) copy-start(bf16[512,192]{0,1:T(8,128)(2,1)} %param.27) | copy-start | bytes 589828

commit v4 on v3

--- a/solution.py
+++ b/solution.py
@@ -139,9 +139,11 @@
 def step_kernel(
     seq_count,
     text_len, step_index, solver_coef,
-    hidden, queries, key_proj, value_proj, norm_gain, norm_bias, positions, frequency, time_embed,
-    gate_table, mod_table, out_weight, proj_weight, proj_bias, latent,
+    norm_gain, norm_bias, positions, frequency, time_embed, proj_bias,
+    value_far, key_far, query_far, gate_far, mod_far, out_far, hidden_far, proj_far, latent_far,
     out,
+    value_proj, key_proj, queries, gate_table, mod_table, out_weight, hidden, proj_weight, latent,
+    load_sem,
     v_send, v_recv, k_send, k_recv, q_send, q_recv, vec, partner_weight, every, part, back, total, gate_full,
     pred_send, pred_recv,
     v_sem, k_sem, q_sem, vec_sem, z_sem, x_sem, core_sem, back_sem, pair_sem,
@@ -156,6 +158,25 @@
     all_rows = seq_count * rows
     own_width = out_weight.shape[0]
 
+    loads = [
+        pltpu.make_async_copy(far, near, load_sem.at[index])
+        for index, (far, near) in enumerate(
+            [
+                (value_far, value_proj),
+                (key_far, key_proj),
+                (query_far, queries),
+                (gate_far, gate_table),
+                (mod_far, mod_table),
+                (out_far, out_weight),
+                (hidden_far, hidden),
+                (proj_far, proj_weight),
+                (latent_far, latent),
+            ]
+        )
+    ]
+    for load in loads:
+        load.start()
+
     barrier = pltpu.get_barrier_semaphore()
 
     def greet(d):
@@ -168,6 +189,7 @@
     pl.semaphore_signal(
         barrier, inc=1, device_id=(1 - cfg, me), device_id_type=pl.DeviceIdType.MESH
     )
+    loads[0].wait()
     for g in range(seq_count):
         v_send[g] = value_proj[:, g * LANES : (g + 1) * LANES]
     lane = lax.broadcasted_iota(jnp.int32, (rows, LANES), 1)
@@ -181,6 +203,7 @@
     sine_part = jnp.sin(angles)
     gain = jnp.concatenate([norm_gain[...], norm_gain[...]], axis=1)
     offset = jnp.concatenate([norm_bias[...], norm_bias[...]], axis=1)
+    loads[1].wait()
     k_send[...] = norm_turn(
         key_proj, gain[1:2], offset[1:2], cosine, sine_part, seq_count, 1.0
     )
@@ -212,10 +235,13 @@
 
     each(seq_count, lambda d: v_copy(d).start(), 1)
     each(seq_count, lambda d: k_copy(d).start(), 1)
+    loads[2].wait()
     q_send[...] = norm_turn(
         queries, gain[0:1], offset[0:1], cosine, sine_part, seq_count, 0.125
     )
     each(seq_count, lambda d: q_copy(d).start(), 1)
+    for load in loads[3:]:
+        load.wait()
     weight_copy = remote(out_weight, partner_weight, pair_sem, 0, (1 - cfg, me))
     weight_copy.start()
     v_recv[me] = v_send[me]
@@ -383,7 +409,13 @@
     vec_width = 256 + mod_table.shape[1]
     out_width = latent.shape[1] // 2
     in_vmem = pl.BlockSpec(memory_space=pltpu.VMEM)
+    in_hbm = pl.BlockSpec(memory_space=pltpu.HBM)
     in_smem = pl.BlockSpec(memory_space=pltpu.SMEM)
+
+    large = [
+        value_proj[0], key_proj[0], queries[0], gate_table.T, mod_table, out_weight.T, hidden[0],
+        proj_weight.T, latent,
+    ]
 
     def sems(count):
         return pltpu.SemaphoreType.DMA((2, count))
@@ -391,9 +423,11 @@
     return pl.pallas_call(
         functools.partial(step_kernel, seq_count),
         out_shape=jax.ShapeDtypeStruct((rows, out_width), f32),
-        in_specs=[in_smem] * 3 + [in_vmem] * 15,
+        in_specs=[in_smem] * 3 + [in_vmem] * 6 + [in_hbm] * 9,
         out_specs=in_vmem,
-        scratch_shapes=[
+        scratch_shapes=[pltpu.VMEM(value.shape, value.dtype) for value in large]
+        + [
+            pltpu.SemaphoreType.DMA((len(large),)),
             pltpu.VMEM((seq_count, rows, LANES), bf16),
             pltpu.VMEM((seq_count, rows, LANES), bf16),
             pltpu.VMEM((seq_count, rows, LANES), bf16),
@@ -420,15 +454,13 @@
             sems(2),
         ],
         compiler_params=pltpu.CompilerParams(
-            collective_id=0, has_side_effects=True, vmem_limit_bytes=40 * 1024 * 1024
+            collective_id=0, has_side_effects=True, vmem_limit_bytes=64 * 1024 * 1024 - 65536
         ),
         name="sampling_step",
     )(
         text_len, step_index, solver_coef,
-        hidden[0], queries[0], key_proj[0], value_proj[0], norm_gain, norm_bias, positions.T,
-        frequency, time_embed[None, :], gate_table.T, mod_table, out_weight.T, proj_weight.T,
-        proj_bias[None, :],
-        latent,
+        norm_gain, norm_bias, positions.T, frequency, time_embed[None, :], proj_bias[None, :],
+        *large,
     )
 
 

time: 81.5 us -> 76.6 us (0.940)
  local copies, waits for them, and re-layouts: 9.13 us -> 3.35 us
  Pallas kernels: 70.4 us -> 71.7 us
    unnamed x33 -> x5, local copies, waits for them, and re-layouts: 8.44 us -> 1.36 us
    pallas_call x1, Pallas kernels: 70.4 us -> 71.7 us  [in_one_kernel(): pl.pallas_call(functools.partial(step_kernel, seq_count), out_shape=jax.S...]
where the time goes in v4:
time: 76.6 us; the launch traced here: 76.3 us
  Pallas kernels  71.7 us (94%)
  local copies, waits for them, and re-layouts  3.35 us (4%)
  between operations  1.32 us (2%)
    pallas_call x1, Pallas kernels, in_one_kernel(): pl.pallas_call(functools.partial(step_kernel, seq_count), out_shape=jax.S...  71.7 us

profile of v4, /device:TPU:3, one launch (start us, length us, event | category | flops | bytes accessed | tf_op | source)
XLA Modules:
  0.0 76.3 jit_solution(18178802004268401742)
XLA Ops:
  1.3 0.0 copy-start.1
  1.3 0.0 copy-start
  1.3 0.7 copy-done.1
  2.0 0.6 broadcast_in_dim.6.time_embed
  2.6 0.0 copy-done
  2.6 0.7 copy.19
  3.3 71.7 %sampling_step.1 = f32[48,32]{1,0:T(8,128)} custom-call(s32[1]{0:T(128)S(6)} %copy.21.text_len, s32[1]{0:T(128)S(6)} %copy.22.step_index, f32[2,50]{1,0:T(2,128)} %solver_coef.1, f32[2,64]{1,0:T(2,128)} %norm_gain.1, f32[2,64]{1,0:T(2,128)} %norm_bias.1, s32[48,3]{1,0:T(8,128)} %bitcast.16, f32[1,128]{1,0:T(1,128)} %constant.2.clone.frequency, ...), custom_call_target="tpu_custom_call" | custom-call | tf_op jit(solution)/shard_map/sampling_step/pallas_call | solution.py:423
  74.9 1.4 %copy.20 = f32[48,32]{0,1:T(8,128)} copy(f32[48,32]{1,0:T(8,128)} %sampling_step.1) | data formatting | bytes 12288 | tf_op jit(solution)/shard_map/sampling_step/pallas_call | solution.py:423
Async XLA Ops:
  1.3 0.7 copy-start.1
  1.3 1.3 %copy-start = (s32[3,48]{1,0:T(4,128)S(1)}, s32[3,48]{1,0:T(4,128)}, u32[]{:S(2)}) copy-start(s32[3,48]{1,0:T(4,128)} %param.24) | copy-start | bytes 1732
